TPU v7x, 512 devices: a whole 4x4x16 slice. The times are simulated.
512 devices in a mesh: ctx: 64 (over z, y_lo, core), head: 8 (over y_hi, x).
Axes of the slice: x: 4, y: 4 (y_hi: 2, y_lo: 2; y = y_hi * 2 + y_lo), z: 16, core: 2. Of those that a mesh axis runs over, the one named last changes fastest.
Arguments:
- span_states: bfloat16 [256, 64, 16384], P('ctx', None, 'head'), may hold values from -6 to 6
- kv_weight: bfloat16 [16384, 2048], P('ctx', 'head'), may hold values from -0.046875 to 0.046875
- q_weight: bfloat16 [16384, 16384], P('ctx', 'head'), may hold values from -0.046875 to 0.046875
- q_scale: float32 [16384], P('head'), may hold values from 0.1 to 1.9
- out_weight: bfloat16 [16384, 16384], P('head', 'ctx'), may hold values from -0.046875 to 0.046875
- decode_states: bfloat16 [2, 64, 16384], P(None, None, 'ctx'), may hold values from -6 to 6
- prior_keys: bfloat16 [64, 256, 1024], P('ctx', None, 'head'), may hold values from -128 to 128
- prior_values: bfloat16 [64, 256, 1024], P('ctx', None, 'head'), may hold values from -6 to 6
- key_scale: float32 [1024], P('head'), may hold values from 0.5 to 2
- cached_len: int32 [64], P('ctx'), may hold values from 1 to 256, as said below
Outputs:
- attn_out: bfloat16 [2, 64, 16384], P(None, 'head', 'ctx')
- new_keys: bfloat16 [64, 256, 1024], P('ctx', None, 'head')
- new_values: bfloat16 [64, 256, 1024], P('ctx', None, 'head')
Inputs may be any that keep to these rules, and one draw needn't show every extreme that they name: `cached_len`: each sequence's cached length; some sequence has the full 256.
All inputs are finite; a program needn't handle non-finite values.
Results may differ from a plain program's by a relative error of at most 0.012.
The roundings to bfloat16 on the way count: a program that leaves them out, or rounds other values in their place, can miss the bound.
Values may be sent and summed in bfloat16 or wider, within the bound.
A program may use at most 64 MiB of HBM per device.

v0:
```python
import jax
import jax.numpy as jnp
from jax import lax
from jax.sharding import PartitionSpec as P


def attend(queries, keys, values, valid):
    scores = jnp.einsum("sgd,skd->sgk", queries, keys, preferred_element_type=jnp.float32)
    scores = jnp.where(valid[:, None, :], scores, jnp.float32(-1e30))
    top = jnp.max(scores, axis=-1, keepdims=True)
    weights = jnp.exp(scores - top)
    total = jnp.sum(weights, axis=-1, keepdims=True)
    mixed = (
        jnp.einsum(
            "sgk,skd->sgd", weights.astype(jnp.bfloat16), values, preferred_element_type=jnp.float32
        )
        / total
    )
    return mixed.astype(jnp.bfloat16)


def body(
    span_states,
    kv_weight,
    q_weight,
    q_scale,
    out_weight,
    decode_states,
    prior_keys,
    prior_values,
    key_scale,
    cached_len,
):
    positions, sequences, _ = span_states.shape
    head_size = key_scale.shape[0]
    group_size = q_scale.shape[0] // head_size
    query_width = q_scale.shape[0]
    steps_count = decode_states.shape[0]
    seq_local = sequences // lax.axis_size("ctx")
    whole_tokens = lax.all_gather(span_states, "head", axis=2, tiled=True)
    flat_tokens = whole_tokens.reshape(positions * sequences, whole_tokens.shape[2])
    block_kv = jnp.dot(
        flat_tokens,
        lax.all_gather(kv_weight, "ctx", axis=0, tiled=True),
        preferred_element_type=jnp.float32,
    )
    stored_keys = (block_kv[:, :head_size] / key_scale).astype(jnp.bfloat16)
    stored_values = block_kv[:, head_size:].astype(jnp.bfloat16)
    packed = jnp.concatenate([stored_keys, stored_values], 1).reshape(
        positions, sequences, 2 * head_size
    )
    arrived = lax.all_to_all(packed, "ctx", split_axis=1, concat_axis=0, tiled=True)
    arrived = jnp.swapaxes(arrived, 0, 1)
    new_keys = arrived[:, :, :head_size]
    new_values = arrived[:, :, head_size:]
    joined_weight = jnp.concatenate([q_weight, kv_weight], 1)
    pieces = []
    for step_index in range(steps_count):

        def project_one(start, count, step_index=step_index):
            picked = decode_states[step_index]
            return jnp.dot(picked, joined_weight, preferred_element_type=jnp.float32)

        pieces.append(
            lax.psum_scatter(
                project_one(jnp.int32(0), seq_local * lax.axis_size("ctx")),
                "ctx",
                scatter_dimension=0,
                tiled=True,
            )
        )
    projected = jnp.stack(pieces, 1)
    query_all = projected[:, :, :query_width] * q_scale
    fresh = projected[:, :, query_width:]
    recent_keys = (fresh[:, :, :head_size] / key_scale).astype(jnp.bfloat16)
    recent_values = fresh[:, :, head_size:].astype(jnp.bfloat16)
    prior_len = prior_keys.shape[1]
    keys_base = jnp.concatenate([prior_keys, new_keys], 1)
    values_base = jnp.concatenate([prior_values, new_values], 1)
    valid_prior = jnp.arange(prior_len, dtype=jnp.int32)[None, :] < cached_len[:, None]
    attended_list = []
    for step_index in range(steps_count):
        scaled = (
            query_all[:, step_index].reshape(seq_local, group_size, head_size)
            * key_scale
            * head_size ** (-0.5)
        )
        scaled = scaled.astype(jnp.bfloat16)
        keys = jnp.concatenate([keys_base, recent_keys[:, : step_index + 1]], 1)
        values = jnp.concatenate([values_base, recent_values[:, : step_index + 1]], 1)
        valid = jnp.concatenate(
            [valid_prior, jnp.ones((seq_local, keys.shape[1] - prior_len), bool)], 1
        )
        attended_list.append(attend(scaled, keys, values, valid).reshape(seq_local, query_width))
    attended = jnp.stack(attended_list, 0)
    results = []
    for step_index in range(steps_count):
        step_partial = jnp.dot(
            lax.all_gather(attended[step_index], "ctx", axis=0, tiled=True),
            out_weight,
            preferred_element_type=jnp.float32,
        )
        results.append(
            lax.psum_scatter(step_partial, "head", scatter_dimension=0, tiled=True).astype(
                jnp.bfloat16
            )
        )
    attn_out = jnp.stack(results, 0)
    return (attn_out, new_keys, new_values)


def solution(mesh):
    return jax.shard_map(
        body,
        mesh=mesh,
        in_specs=(
            P("ctx", None, "head"),
            P("ctx", "head"),
            P("ctx", "head"),
            P("head"),
            P("head", "ctx"),
            P(None, None, "ctx"),
            P("ctx", None, "head"),
            P("ctx", None, "head"),
            P("head"),
            P("ctx"),
        ),
        out_specs=(P(None, "head", "ctx"), P("ctx", None, "head"), P("ctx", None, "head")),
        check_vma=False,
    )
```

profile of v0, /device:TPU:1, one launch (start us, length us, event | category | flops | bytes accessed | tf_op | source)
XLA Modules:
  0.0 762.6 jit_solution(8820422009545449133)
XLA Ops:
  8.0 0.0 copy-start
  8.0 0.0 copy-start.1
  8.0 0.0 copy-start.2
  8.0 0.0 all-reduce.7.cloned.1.call-start
  8.1 1.4 constant_dynamic-update-slice_fusion.1
  9.5 0.0 copy-done.1
  9.5 0.0 copy-done.2
  9.5 1.2 convolution_bitcast_fusion.1
  10.7 1.2 convolution_bitcast_fusion
  11.9 0.0 copy-start.5
  11.9 0.0 all-reduce.7.cloned.1.call-update
  11.9 0.0 all-gather.5.cloned.1.call-start
  11.9 0.5 all-gather.5.cloned.1.call-update
  12.5 0.0 all-gather.7.cloned.1.call-start
  12.5 0.5 all-gather.7.cloned.1.call-update
  13.7 1.3 dynamic-slice
  15.0 467.9 %all-reduce.7.cloned.1.call-done = (f32[64,2304]{1,0:T(8,128)}, f32[64,2304]{1,0:T(8,128)}) async-done(((f32[64,2304]{1,0:T(8,128)}, f32[64,2304]{1,0:T(8,128)}), (f32[64,2304]{1,0:T(8,128)}, f32[64,2304]{1,0:T(8,128)})) %all-reduce.7.cloned.1.call-update) | async-done | bytes 1179664
  482.9 1.6 dynamic-slice_bitcast_fusion
  484.5 0.0 copy-done.5
  484.5 0.0 all-gather.5.cloned.1.call-done
  484.5 0.0 all-gather.7.cloned.1.call-done
  484.6 0.0 copy-start.6
  484.6 9.1 %fusion.52 = f32[256,256]{0,1:T(8,128)S(1)} fusion(bf16[256,16384]{1,0:T(8,128)(2,1)} %bitcast.68, bf16[16384,256]{1,0:T(8,128)(2,1)} %all-gather.7.cloned.1.call-done), kind=kOutput, calls=%fused_computation.85 | convolution fusion | flops 2147483648 | bytes 17039360 | tf_op jit(solution)/shard_map/dot_general | solution.py:42
  493.7 0.0 copy-start.7
  493.7 0.0 copy-start.8
  493.8 0.0 copy-done.6
  493.8 0.1 fusion.24
  493.9 0.1 copy.21
  494.0 0.8 copy.22
  494.7 11.9 %all-to-all-start = ((bf16[4,64,256]{2,0,1:T(4,128)(2,1)}), bf16[4,64,256]{2,0,1:T(4,128)(2,1)S(1)}, u32[]{:S(2)}, u32[]{:S(2)}) async-start(bf16[4,64,256]{2,0,1:T(4,128)(2,1)} %copy.22), calls=%async_computation | async-start | bytes 262144 | tf_op jit(solution)/shard_map/all_to_all | solution.py:52
  506.6 0.0 reduce-scatter.5.cloned.1.call-start
  506.8 0.1 convert_reduce_fusion.1
  506.8 16.9 %all-to-all-done = bf16[4,64,256]{2,0,1:T(4,128)(2,1)S(1)} async-done(((bf16[4,64,256]{2,0,1:T(4,128)(2,1)}), bf16[4,64,256]{2,0,1:T(4,128)(2,1)S(1)}, u32[]{:S(2)}, u32[]{:S(2)}) %all-to-all-start) | async-done | bytes 131104 | tf_op jit(solution)/shard_map/all_to_all | solution.py:52
  523.8 0.0 copy-start.3
  523.8 0.0 copy-start.4
  523.8 0.0 copy-done.7
  523.8 0.3 fusion.51
  524.1 0.2 fusion.25
  524.3 0.0 copy-done.8
  524.3 0.2 fusion
  524.5 0.3 fusion.50
  524.8 0.2 fusion.27
  525.0 0.2 fusion.1
  525.2 62.0 %all-gather.1 = bf16[64,1,2048]{2,1,0:T(2,128)(2,1)S(1)} all-gather(bf16[1,1,2048]{2,1,0:T(2,128)(2,1)S(1)} %reshape.135), channel_id=1, replica_groups=mesh['ctx'=64,'head'=8] {'ctx'}, dimensions={0}, use_global_device_ids=true | all-gather | bytes 266240 | tf_op jit(solution)/shard_map/all_gather | solution.py:99
  587.2 0.0 copy-done
  587.2 0.9 fusion.2
  588.2 0.0 copy-done.3
  588.2 0.0 copy-done.4
  588.2 0.0 reduce-scatter.5.cloned.1.call-update
  588.2 0.0 reduce-scatter.3.cloned.1.call-start
  588.3 61.5 %all-gather = bf16[64,1,2048]{2,1,0:T(2,128)(2,1)S(1)} all-gather(bf16[1,1,2048]{2,1,0:T(2,128)(2,1)S(1)} %reshape.133), channel_id=1, replica_groups=mesh['ctx'=64,'head'=8] {'ctx'}, dimensions={0}, use_global_device_ids=true | all-gather | bytes 266240 | tf_op jit(solution)/shard_map/all_gather | solution.py:99
  649.8 0.9 fusion.5
  650.7 0.0 reduce-scatter.3.cloned.1.call-update
  650.8 13.5 %reduce-scatter.5.cloned.1.call-done = f32[8,256]{1,0:T(8,128)} async-done(((f32[64,256]{1,0:T(8,128)}), f32[8,256]{1,0:T(8,128)}) %reduce-scatter.5.cloned.1.call-update) | async-done | bytes 8208 | tf_op jit(solution)/shard_map/reduce_scatter | solution.py:104
  664.3 0.7 convert_bitcast_fusion
  665.0 88.7 %reduce-scatter.3.cloned.1.call-done = f32[8,256]{1,0:T(8,128)} async-done(((f32[64,256]{1,0:T(8,128)}), f32[8,256]{1,0:T(8,128)}) %reduce-scatter.3.cloned.1.call-update) | async-done | bytes 8208 | tf_op jit(solution)/shard_map/reduce_scatter | solution.py:104
  753.7 0.7 convert_bitcast_fusion.1
  754.4 0.6 pad_maximum_fusion.2
  (16 shorter events, 0.2 us)
Async XLA Ops:
  8.0 579.2 %copy-start = (bf16[2048,256]{1,0:T(8,128)(2,1)S(1)}, bf16[2048,256]{1,0:T(8,128)(2,1)}, u32[]{:S(2)}) copy-start(bf16[2048,256]{1,0:T(8,128)(2,1)} %param.14) | copy-start | bytes 3145732
  8.0 1.5 copy-start.1
  8.0 1.5 copy-start.2
  8.0 474.9 %all-reduce.7.cloned.1.call-start = ((), (), s32[]{:S(2)}) async-start(), calls=%async_computation.7 | async-start | bytes 2359296
  11.9 472.6 %copy-start.5 = (f32[2048]{0:T(1024)S(1)}, f32[2048]{0:T(1024)}, u32[]{:S(2)}) copy-start(f32[2048]{0:T(1024)} %param.13) | copy-start | bytes 24580
  11.9 472.7 %all-gather.5.cloned.1.call-start = ((), (), s32[]{:S(2)}) async-start(), calls=%async_computation.3 | async-start | bytes 9437184 | tf_op jit(solution)/shard_map/all_gather | solution.py:40
  12.5 472.1 %all-gather.7.cloned.1.call-start = ((), (), s32[]{:S(2)}) async-start(), calls=%async_computation.4 | async-start | bytes 8519680 | tf_op jit(solution)/shard_map/all_gather | solution.py:44
  484.6 9.2 %copy-start.6 = (f32[128]{0:T(128)S(1)}, f32[128]{0:T(128)}, u32[]{:S(2)}) copy-start(f32[128]{0:T(128)} %param.18) | copy-start | bytes 1540
  493.7 30.1 %copy-start.7 = (bf16[1,256,128]{2,1,0:T(8,128)(2,1)S(1)}, bf16[1,256,128]{2,1,0:T(8,128)(2,1)}, u32[]{:S(2)}) copy-start(bf16[1,256,128]{2,1,0:T(8,128)(2,1)} %param.16) | copy-start | bytes 196612
  493.7 30.6 %copy-start.8 = (bf16[1,256,128]{2,1,0:T(8,128)(2,1)S(1)}, bf16[1,256,128]{2,1,0:T(8,128)(2,1)}, u32[]{:S(2)}) copy-start(bf16[1,256,128]{2,1,0:T(8,128)(2,1)} %param.17) | copy-start | bytes 196612
  494.7 29.0 %all-to-all-start = ((bf16[4,64,256]{2,0,1:T(4,128)(2,1)}), bf16[4,64,256]{2,0,1:T(4,128)(2,1)S(1)}, u32[]{:S(2)}, u32[]{:S(2)}) async-start(bf16[4,64,256]{2,0,1:T(4,128)(2,1)} %copy.22), calls=%async_computation | async-start | bytes 262144 | tf_op jit(solution)/shard_map/all_to_all | solution.py:52
  506.6 157.6 %reduce-scatter.5.cloned.1.call-start = ((), (), s32[]{:S(2)}) async-start(), calls=%async_computation.6 | async-start | bytes 73728 | tf_op jit(solution)/shard_map/reduce_scatter | solution.py:104
  523.8 64.4 %copy-start.3 = (bf16[1,256,128]{2,1,0:T(8,128)(2,1)}, bf16[1,256,128]{2,1,0:T(8,128)(2,1)S(1)}, u32[]{:S(2)}) copy-start(bf16[1,256,128]{2,1,0:T(8,128)(2,1)S(1)} %get-tuple-element.7) | copy-start | bytes 196612
  523.8 64.4 %copy-start.4 = (bf16[1,256,128]{2,1,0:T(8,128)(2,1)}, bf16[1,256,128]{2,1,0:T(8,128)(2,1)S(1)}, u32[]{:S(2)}) copy-start(bf16[1,256,128]{2,1,0:T(8,128)(2,1)S(1)} %get-tuple-element.8) | copy-start | bytes 196612
  588.2 165.5 %reduce-scatter.3.cloned.1.call-start = ((), (), s32[]{:S(2)}) async-start(), calls=%async_computation.5 | async-start | bytes 73728 | tf_op jit(solution)/shard_map/reduce_scatter | solution.py:104
Sparse Core Ops, SparseCore 0:
  12.0 470.8 all-reduce.6
Sparse Core Ops, SparseCore 1:
  15.6 129.4 all-gather.4
  147.1 128.7 all-gather.6
  588.3 75.9 reduce-scatter.4
  669.4 84.3 reduce-scatter.2
where the time goes:
time: 764 us; the launch traced here: 763 us
  waiting for transfers between devices  588 us (77%)
  blocking collectives  124 us (16%)
  between operations  16.6 us (2%)
  matrix products  14.3 us (2%)
  starting transfers between devices  12.1 us (2%)
    unnamed x6, waiting for transfers between devices  469 us
    all_gather x2, blocking collectives, body(): lax.all_gather(attended[step_index], 'ctx', axis=0, tiled=True)  124 us
    reduce_scatter x2, waiting for transfers between devices, body(): lax.psum_scatter(step_partial, 'head', scatter_dimension=0, tiled=True)  102 us
    all_to_all x1, waiting for transfers between devices, body(): lax.all_to_all(packed, 'ctx', split_axis=1, concat_axis=0, tiled=True)  16.9 us
  transfers between devices with their start and end apart: 6, of which 4 were waited for; matrix products, arithmetic and copies ran while one was open for 1% of the time, Pallas kernels for 0%

commit v1 on v0

v1 whole, which is shorter than its diff:
```python
import functools

import jax
import jax.numpy as jnp
from jax import lax
from jax.experimental import pallas as pl
from jax.experimental.pallas import tpu as pltpu
from jax.sharding import PartitionSpec as P

MESH = pl.DeviceIdType.MESH
G = 4
F32 = jnp.float32
BF16 = jnp.bfloat16


def onehot(rows, cols, source):
    r = lax.broadcasted_iota(jnp.int32, (rows, cols), 0)
    k = lax.broadcasted_iota(jnp.int32, (rows, cols), 1)
    return jnp.where(k == source(r), 1.0, 0.0).astype(BF16)


def dot(a, b):
    return jnp.dot(a, b, preferred_element_type=F32)


def dot_t(a, b):
    return lax.dot_general(a, b, (((1,), (1,)), ((), ())), preferred_element_type=F32)


def kernel(
    nz, nh,
    span_ref, kvw_ref, qw_ref, qs_ref, ow_ref, dec_ref, pk_ref, pv_ref, ks_ref, cl_ref,
    out_ref, nk_ref, nv_ref,
    spanbuf, wbuf, part, rsbuf, a2abuf, kvnew,
    qbuf, qrecv1, qrecv2, qrow, qup, qdn, qsc, fk, fv,
    gath, gf, lhs, obuf, orecv,
    perm_s, w_r, up_s, dn_s,
    spc_s, spc_r, spy_s, spy_r, spf_s, spf_r,
    q1_s, q1_r, q2_s, q2_r, qu_s, qu_r, qd_s, qd_r,
    rs_s, rs_r, a2_s, a2_r, ga_s, ga_r, gy_s, gy_r, gc_s, gc_r, or_s, or_r,
):
    hpg = nh // G
    up_n, dn_n = nz // 2, nz // 2 - 1
    positions, seqs, feats = span_ref.shape
    hd = ks_ref.shape[1]
    group = qs_ref.shape[0]
    steps = dec_ref.shape[0] // seqs
    qcols = group * hd
    blk = positions * nz
    crows = kvw_ref.shape[0] // hpg
    c, h = lax.axis_index("ctx"), lax.axis_index("head")
    z, g = c // G, c % G
    yl, co = g // 2, g % 2
    core_dev = (z * G + yl * 2 + (1 - co), h)
    y_dev = (z * G + (1 - yl) * 2 + co, h)
    up_dev = (lax.rem(z + 1, nz) * G + g, h)
    dn_dev = (lax.rem(z + nz - 1, nz) * G + g, h)

    def zmod(a):
        return lax.rem(a + 2 * nz, nz)

    def rc(src, dst, ss, rs, dev):
        return pltpu.make_async_remote_copy(
            src_ref=src, dst_ref=dst, send_sem=ss, recv_sem=rs, device_id=dev, device_id_type=MESH
        )

    def other(dev):
        return jnp.logical_or(dev[0] != c, dev[1] != h)

    per = (G * nz) // nh

    def perm_to(r):
        zeta = lax.rem(c, per) * hpg + r
        return (zeta * G + h // hpg, c // per), zeta

    def perm_from(p):
        return (h * per + z // hpg, g * hpg + p)

    def rs_to(d):
        return (z * G + d % G, g * hpg + d // G)

    def rs_from(hs):
        return (z * G + h // hpg, hs)

    barrier = pltpu.get_barrier_semaphore()

    def greet(dev):
        pl.semaphore_signal(barrier, inc=1, device_id=dev, device_id_type=MESH)

    greet(core_dev)
    greet(y_dev)

    def greet_z(i, _):
        greet((zmod(z + i) * G + g, h))
        return 0

    def greet_h(i, _):
        greet((c, lax.rem(h + i, nh)))
        return 0

    lax.fori_loop(1, nz, greet_z, 0)
    lax.fori_loop(1, nh, greet_h, 0)
    for p in range(hpg):
        dev = perm_from(p)

        @pl.when(other(dev))
        def _():
            greet(dev)

    def greet_rs(hs, _):
        dev = rs_from(hs)

        @pl.when(other(dev))
        def _():
            greet(dev)

        return 0

    lax.fori_loop(0, nh, greet_rs, 0)

    order = onehot(seqs, seqs, lambda r: (r % nz) * G + r // nz)
    for p in range(positions):
        rows = dot(order, span_ref[p]).astype(BF16)
        for k in range(G):
            spanbuf[k, g, p * nz:(p + 1) * nz, :] = rows[k * nz:(k + 1) * nz]

    nrow = steps * seqs
    pick = onehot(
        nrow, nrow,
        lambda r: (r % steps) * seqs
        + ((r // steps) % nz) * G + ((r // (steps * nz)) % 2) * 2 + r // (steps * nz * 2),
    )
    decp = dot(pick, dec_ref[...]).astype(BF16)
    half = nrow // 2
    for k in range(2):
        qbuf[k, :, 0:qcols] = dot(decp[k * half:(k + 1) * half], qw_ref[...])
        qbuf[k, :, qcols:] = dot(decp[k * half:(k + 1) * half], kvw_ref[...])

    peers = 2 + (nz - 1) + (nh - 1)
    for r in range(hpg):
        peers = peers + jnp.where(other(perm_to(r)[0]), 1, 0)
    for d in range(nh):
        peers = peers + jnp.where(other(rs_to(d)), 1, 0)
    pl.semaphore_wait(barrier, peers)

    def wslot(p, zeta):
        return wbuf.at[p, pl.ds(pl.multiple_of(zeta * crows, crows), crows), :]

    def perm_copy(r):
        dev, zeta = perm_to(r)
        p = h % hpg
        return rc(kvw_ref.at[pl.ds(r * crows, crows), :], wslot(p, zeta), perm_s.at[r], w_r.at[p, zeta], dev), dev

    for r in range(hpg):
        copy, dev = perm_copy(r)

        @pl.when(other(dev))
        def _():
            copy.start()

        @pl.when(jnp.logical_not(other(dev)))
        def _():
            wslot(h % hpg, z)[...] = kvw_ref[r * crows:(r + 1) * crows, :]

    q1 = rc(qbuf.at[1 - co], qrecv1, q1_s, q1_r, core_dev)
    q1.start()
    spc = rc(spanbuf.at[:, g], spanbuf.at[:, g], spc_s, spc_r, core_dev)
    spc.start()
    q1.wait_recv()
    qh = half // 2
    for k in range(2):
        qbuf[co, k * qh:(k + 1) * qh, :] = qbuf[co, k * qh:(k + 1) * qh, :] + qrecv1[k * qh:(k + 1) * qh, :]
    q2 = rc(qbuf.at[co, pl.ds(pl.multiple_of((1 - yl) * qh, qh), qh), :], qrecv2, q2_s, q2_r, y_dev)
    q2.start()

    def spy(k):
        return rc(spanbuf.at[k, g], spanbuf.at[k, g], spy_s.at[k], spy_r.at[k], y_dev)

    def spf(k):
        gy = (1 - yl) * 2 + co
        return rc(spanbuf.at[k, gy], spanbuf.at[k, gy], spf_s.at[k], spf_r.at[k], core_dev)

    for k in range(G):
        spy(k).start()
    q2.wait_recv()
    own = qbuf[co, pl.ds(pl.multiple_of(yl * qh, qh), qh), :] + qrecv2[...]
    for r in range(qh):
        qrow[r, 0:1, :] = own[r:r + 1, :]

    def recv_w(p, zeta):
        rc(wslot(p, zeta), wslot(p, zeta), up_s.at[0, 0], w_r.at[p, zeta], up_dev).wait_recv()

    def send_up(s, p):
        zeta = zmod(z - s)
        return rc(wslot(p, zeta), wslot(p, zeta), up_s.at[s, p], w_r.at[p, zeta], up_dev)

    def send_dn(s, p):
        zeta = zmod(z + s)
        return rc(wslot(p, zeta), wslot(p, zeta), dn_s.at[s, p], w_r.at[p, zeta], dn_dev)

    def qpart(d):
        return qrow.at[pl.ds(d * steps, steps)]

    for p in range(hpg):
        dev = perm_from(p)

        @pl.when(other(dev))
        def _():
            recv_w(p, z)

        send_up(0, p).start()
        send_dn(0, p).start()

    def q_up(s):
        src = qpart(zmod(z + up_n)) if s == 0 else qup.at[s - 1]
        return rc(src, qup.at[s], qu_s.at[s], qu_r.at[s], up_dev)

    def q_dn(s):
        src = qpart(zmod(z - dn_n)) if s == 0 else qdn.at[s - 1]
        return rc(src, qdn.at[s], qd_s.at[s], qd_r.at[s], dn_dev)

    q_up(0).start()
    q_dn(0).start()
    for s in range(1, up_n):
        for p in range(hpg):
            recv_w(p, zmod(z - s))
            send_up(s, p).start()
            if s <= dn_n:
                recv_w(p, zmod(z + s))
            if s < dn_n:
                send_dn(s, p).start()
        q_up(s - 1).wait_recv()
        qup[s - 1] = qup[s - 1] + qpart(zmod(z + up_n - s))[...]
        q_up(s).start()
        if s < dn_n:
            q_dn(s - 1).wait_recv()
            qdn[s - 1] = qdn[s - 1] + qpart(zmod(z - dn_n + s))[...]
            q_dn(s).start()
        if s in (3, 5, 6):
            k = (3, 5, 6).index(s)
            spy(k).wait_recv()
            spf(k).start()
    for k in range(G):
        if k not in [(3, 5, 6).index(s) for s in range(1, up_n) if s in (3, 5, 6)]:
            spy(k).wait_recv()
            spf(k).start()
    for p in range(hpg):
        recv_w(p, zmod(z - up_n))
    spc.wait_recv()
    for k in range(G):
        spf(k).wait_recv()

    def rs_copy(d):
        return rc(part.at[d], rsbuf.at[h], rs_s.at[d], rs_r.at[h], rs_to(d))

    def product(i, _):
        d = lax.rem(i + h, nh)
        tile = spanbuf[d % G].reshape(G * blk, feats)
        part[d] = dot(tile, wbuf[d // G]).astype(BF16)
        away = other(rs_to(d))

        @pl.when(away)
        def _():
            rs_copy(d).start()

        @pl.when(jnp.logical_not(away))
        def _():
            rsbuf[h] = part[d]

        return 0

    lax.fori_loop(0, nh, product, 0)

    q_up(up_n - 1).wait_recv()
    q_dn(dn_n - 1).wait_recv()
    qv = qpart(z)[...] + qup[up_n - 1] + qdn[dn_n - 1]
    ks = ks_ref[...]
    fk[...] = jnp.zeros_like(fk)
    fv[...] = jnp.zeros_like(fv)
    for t in range(steps):
        for j in range(group):
            qsc[t * group + j:t * group + j + 1, :] = qv[t, 0:1, j * hd:(j + 1) * hd]
        fk[t:t + 1, :] = qv[t, 0:1, qcols:qcols + hd] / ks
        fv[t:t + 1, :] = qv[t, 0:1, qcols + hd:qcols + 2 * hd]
    scale = jnp.concatenate([qs_ref[...]] * steps, 0)
    scaled = (qsc[...] * scale * ks * (hd ** -0.5)).astype(BF16)
    s_old = dot_t(scaled, pk_ref[...])
    where = lax.broadcasted_iota(jnp.int32, s_old.shape, 1)
    s_old = jnp.where(where < cl_ref[0], s_old, -1e30)
    s_fresh = dot_t(scaled, fk[...].astype(BF16))
    col = lax.broadcasted_iota(jnp.int32, s_fresh.shape, 1)
    row = lax.broadcasted_iota(jnp.int32, s_fresh.shape, 0)
    s_fresh = jnp.where(col <= row // group, s_fresh, -1e30)
    top0 = jnp.maximum(jnp.max(s_old, 1, keepdims=True), jnp.max(s_fresh, 1, keepdims=True))

    for hs in range(nh):
        @pl.when(other(rs_from(hs)))
        def _():
            rc(rsbuf.at[hs], rsbuf.at[hs], rs_s.at[0], rs_r.at[hs], core_dev).wait_recv()

    total_kv = rsbuf[0].astype(F32)
    for hs in range(1, nh):
        total_kv = total_kv + rsbuf[hs].astype(F32)
    stored = jnp.concatenate([total_kv[:, :hd] / ks, total_kv[:, hd:]], 1).astype(BF16)
    pos = G * positions
    spread = onehot(G * blk, G * blk, lambda r: (r % pos) * nz + r // pos)
    a2abuf[...] = dot(spread, stored).astype(BF16).reshape(a2abuf.shape)

    def a2_copy(i):
        zt = zmod(z + i)
        return rc(a2abuf.at[zt], kvnew.at[z], a2_s.at[i], a2_r.at[z], (zt * G + g, h))

    def a2_start(i, _):
        a2_copy(i).start()
        return 0

    lax.fori_loop(1, nz, a2_start, 0)
    kvnew[z] = a2abuf[z]

    def a2_wait(i, _):
        zt = zmod(z + i)
        rc(kvnew.at[zt], kvnew.at[zt], a2_s.at[0], a2_r.at[zt], core_dev).wait_recv()
        return 0

    lax.fori_loop(1, nz, a2_wait, 0)
    kv = kvnew[...].reshape(nz * pos, 2 * hd)
    k_new, v_new = kv[:, :hd], kv[:, hd:]
    nk_ref[...] = k_new
    nv_ref[...] = v_new

    s_new = dot_t(scaled, k_new)
    top = jnp.maximum(top0, jnp.max(s_new, 1, keepdims=True))
    w_old, w_new, w_fresh = jnp.exp(s_old - top), jnp.exp(s_new - top), jnp.exp(s_fresh - top)
    total = (
        jnp.sum(w_old, 1, keepdims=True) + jnp.sum(w_new, 1, keepdims=True) + jnp.sum(w_fresh, 1, keepdims=True)
    )
    mixed = (
        dot(w_old.astype(BF16), pv_ref[...]) + dot(w_new.astype(BF16), v_new)
        + dot(w_fresh.astype(BF16), fv[...].astype(BF16))
    ) / total
    gath[z, g] = mixed.astype(BF16)

    def ga_copy(i):
        return rc(gath.at[z, g], gath.at[z, g], ga_s.at[i], ga_r.at[z], (zmod(z + i) * G + g, h))

    def ga_start(i, _):
        ga_copy(i).start()
        return 0

    lax.fori_loop(1, nz, ga_start, 0)

    def ga_wait(i, _):
        zt = zmod(z + i)
        rc(gath.at[zt, g], gath.at[zt, g], ga_s.at[0], ga_r.at[zt], core_dev).wait_recv()
        return 0

    lax.fori_loop(1, nz, ga_wait, 0)
    gy = rc(gath.at[:, g], gath.at[:, g], gy_s, gy_r, y_dev)
    gy.start()

    def gc_copy(k):
        gk = g if k == 0 else (1 - yl) * 2 + co
        return rc(gath.at[:, gk], gath.at[:, gk], gc_s.at[k], gc_r.at[k], core_dev)

    gc_copy(0).start()
    gy.wait_recv()
    gc_copy(1).start()
    gc_copy(0).wait_recv()
    gc_copy(1).wait_recv()

    gf[...] = gath[...].reshape(gf.shape).astype(F32)
    for t in range(steps):
        for j in range(group):
            rows = gf[pl.ds(t * group + j, seqs, stride=steps * group), :]
            lhs[t * seqs:(t + 1) * seqs, j * hd:(j + 1) * hd] = rows.astype(BF16)
    obuf[...] = dot(lhs[...], ow_ref[...]).reshape(obuf.shape)
    mine = seqs // nh

    def or_copy(i):
        ht = lax.rem(h + i, nh)
        src = obuf.at[:, pl.ds(pl.multiple_of(ht * mine, mine), mine), :]
        return rc(src, orecv.at[h], or_s.at[i], or_r.at[h], (c, ht))

    def or_start(i, _):
        or_copy(i).start()
        return 0

    lax.fori_loop(1, nh, or_start, 0)
    orecv[h] = obuf[:, pl.ds(pl.multiple_of(h * mine, mine), mine), :]

    def or_wait(i, _):
        hs = lax.rem(h + i, nh)
        rc(orecv.at[hs], orecv.at[hs], or_s.at[0], or_r.at[hs], core_dev).wait_recv()
        return 0

    lax.fori_loop(1, nh, or_wait, 0)
    result = orecv[0]
    for hs in range(1, nh):
        result = result + orecv[hs]
    out_ref[...] = result.astype(BF16)

    for r in range(hpg):
        copy, dev = perm_copy(r)

        @pl.when(other(dev))
        def _():
            copy.wait_send()

    q1.wait_send()
    q2.wait_send()
    spc.wait_send()
    for k in range(G):
        spy(k).wait_send()
        spf(k).wait_send()
    for s in range(up_n):
        for p in range(hpg):
            send_up(s, p).wait_send()
            if s < dn_n:
                send_dn(s, p).wait_send()
        q_up(s).wait_send()
        if s < dn_n:
            q_dn(s).wait_send()

    def rs_done(d, _):
        @pl.when(other(rs_to(d)))
        def _():
            rs_copy(d).wait_send()

        return 0

    lax.fori_loop(0, nh, rs_done, 0)

    def z_done(i, _):
        a2_copy(i).wait_send()
        ga_copy(i).wait_send()
        return 0

    lax.fori_loop(1, nz, z_done, 0)
    gy.wait_send()
    gc_copy(0).wait_send()
    gc_copy(1).wait_send()

    def or_done(i, _):
        or_copy(i).wait_send()
        return 0

    lax.fori_loop(1, nh, or_done, 0)


def body(
    span_states, kv_weight, q_weight, q_scale, out_weight, decode_states, prior_keys, prior_values, key_scale, cached_len
):
    nh = lax.axis_size("head")
    nz = lax.axis_size("ctx") // G
    hpg = nh // G
    positions, seqs, feats = span_states.shape
    hd = key_scale.shape[0]
    qcols = q_scale.shape[0]
    group = qcols // hd
    steps, _, depth = decode_states.shape
    width = qcols + 2 * hd
    nrow = steps * seqs
    blk = positions * nz
    pos = G * positions
    ocols = out_weight.shape[1]
    prior = prior_keys.shape[1]
    vm = pltpu.VMEM
    dma = pltpu.SemaphoreType.DMA
    up_n, dn_n = nz // 2, nz // 2 - 1
    vspec = pl.BlockSpec(memory_space=pltpu.VMEM)
    out, nk, nv = pl.pallas_call(
        functools.partial(kernel, nz, nh),
        out_shape=(
            jax.ShapeDtypeStruct((steps, seqs // nh, ocols), BF16),
            jax.ShapeDtypeStruct((nz * pos, hd), BF16),
            jax.ShapeDtypeStruct((nz * pos, hd), BF16),
        ),
        in_specs=[vspec] * 9 + [pl.BlockSpec(memory_space=pltpu.SMEM)],
        out_specs=(vspec,) * 3,
        scratch_shapes=[
            vm((G, G, blk, feats), BF16),
            vm((hpg, feats, 2 * hd), BF16),
            vm((nh, G * blk, 2 * hd), BF16),
            vm((nh, G * blk, 2 * hd), BF16),
            vm((nz, pos, 2 * hd), BF16),
            vm((nz, pos, 2 * hd), BF16),
            vm((2, nrow // 2, width), F32),
            vm((nrow // 2, width), F32),
            vm((nrow // 4, width), F32),
            vm((nrow // 4, 1, width), F32),
            vm((up_n, steps, 1, width), F32),
            vm((dn_n, steps, 1, width), F32),
            vm((steps * group, hd), F32),
            vm((16, hd), F32),
            vm((16, hd), F32),
            vm((nz, G, steps * group, hd), BF16),
            vm((seqs * steps * group, hd), F32),
            vm((nrow, qcols), BF16),
            vm((steps, seqs, ocols), F32),
            vm((nh, steps, seqs // nh, ocols), F32),
            dma((hpg,)), dma((hpg, nz)), dma((up_n, hpg)), dma((dn_n, hpg)),
            dma, dma, dma((G,)), dma((G,)), dma((G,)), dma((G,)),
            dma, dma, dma, dma, dma((up_n,)), dma((up_n,)), dma((dn_n,)), dma((dn_n,)),
            dma((nh,)), dma((nh,)), dma((nz,)), dma((nz,)), dma((nz,)), dma((nz,)),
            dma, dma, dma((2,)), dma((2,)), dma((nh,)), dma((nh,)),
        ],
        compiler_params=pltpu.CompilerParams(
            collective_id=0, has_side_effects=True, vmem_limit_bytes=40 * 2**20
        ),
        name="layer",
    )(
        span_states, kv_weight, q_weight, q_scale.reshape(group, hd), out_weight,
        decode_states.reshape(nrow, depth), prior_keys.reshape(prior, hd), prior_values.reshape(prior, hd),
        key_scale.reshape(1, hd), cached_len,
    )
    return out, nk.reshape(1, nz * pos, hd), nv.reshape(1, nz * pos, hd)


def solution(mesh):
    return jax.shard_map(
        body,
        mesh=mesh,
        in_specs=(
            P("ctx", None, "head"),
            P("ctx", "head"),
            P("ctx", "head"),
            P("head"),
            P("head", "ctx"),
            P(None, None, "ctx"),
            P("ctx", None, "head"),
            P("ctx", None, "head"),
            P("head"),
            P("ctx"),
        ),
        out_specs=(P(None, "head", "ctx"), P("ctx", None, "head"), P("ctx", None, "head")),
        check_vma=False,
    )
```

time: 764 us -> 127 us (0.17)
  waiting for transfers between devices: 588 us -> 0 us
  blocking collectives: 124 us -> 0 us
  Pallas kernels: 0 us -> 116 us
  between operations: 16.6 us -> 1.33 us
  matrix products: 14.3 us -> 0 us
  starting transfers between devices: 12.1 us -> 0 us
    unnamed x6 -> x0, waiting for transfers between devices: 469 us -> none
    all_gather x2 -> x0, blocking collectives: 124 us -> none  [body(): lax.all_gather(attended[step_index], 'ctx', axis=0, tiled=True)]
    pallas_call x0 -> x1, Pallas kernels: none -> 116 us  [body(): pl.pallas_call(functools.partial(kernel, nz, nh), out_shape=(jax.ShapeDty...]
    reduce_scatter x2 -> x0, waiting for transfers between devices: 102 us -> none  [body(): lax.psum_scatter(step_partial, 'head', scatter_dimension=0, tiled=True)]
    all_to_all x1 -> x0, waiting for transfers between devices: 16.9 us -> none  [body(): lax.all_to_all(packed, 'ctx', split_axis=1, concat_axis=0, tiled=True)]
    dot_general x9 -> x0, matrix products: 14.3 us -> none  [the longest x1 9.13 us: body(): jnp.dot(flat_tokens, lax.all_gather(kv_weight, 'ctx', axis=0, tiled=True)...]
    all_to_all x1 -> x0, starting transfers between devices: 11.9 us -> none  [body(): lax.all_to_all(packed, 'ctx', split_axis=1, concat_axis=0, tiled=True)]
  transfers between devices with their start and end apart: 6 -> 0, of which waited for: 4 -> 0; matrix products, arithmetic and copies ran while one was open for 1% -> 0% of each run, Pallas kernels for 0% -> 0%
where the time goes in v1:
time: 127 us
  Pallas kernels  116 us (91%)
  local copies, waits for them, and re-layouts  9.6 us (8%)
  between operations  1.33 us (1%)
    pallas_call x1, Pallas kernels, body(): pl.pallas_call(functools.partial(kernel, nz, nh), out_shape=(jax.ShapeDty...  116 us
    unnamed x21, local copies, waits for them, and re-layouts  9.6 us

profile of v1, /device:TPU:1, one launch (start us, length us, event | category | flops | bytes accessed | tf_op | source)
XLA Modules:
  0.0 126.7 jit_solution(6415267476707636827)
XLA Ops:
  0.6 0.0 copy-start.7
  1.3 0.0 copy-start.8
  1.3 0.0 copy-done.7
  1.3 0.6 copy-done.8
  2.0 0.0 copy-start
  2.0 1.2 copy-done
  3.2 0.0 copy-start.1
  3.2 1.2 copy-done.1
  4.4 0.0 copy-start.2
  4.4 1.2 copy-done.2
  5.6 0.0 copy-start.3
  5.6 0.9 copy-done.3
  6.5 0.0 copy-start.4
  6.5 0.8 copy-done.4
  7.4 0.0 copy-start.5
  7.4 0.8 copy-done.5
  8.2 0.0 copy-start.6
  8.2 0.8 copy-done.6
  9.1 115.8 %layer.1 = (bf16[2,8,256]{2,1,0:T(8,128)(2,1)S(1)}, bf16[256,128]{1,0:T(8,128)(2,1)S(1)}, bf16[256,128]{1,0:T(8,128)(2,1)S(1)}) custom-call(bf16[4,64,2048]{2,1,0:T(8,128)(2,1)S(1)} %copy-done, bf16[256,256]{1,0:T(8,128)(2,1)S(1)} %copy-done.3, bf16[256,2048]{1,0:T(8,128)(2,1)S(1)} %copy-done.1, f32[16,128]{1,0:T(8,128)S(1)} %bitcast.12, ...), custom_call_target="tpu_custom_call" | custom-call | tf_op jit(solution)/shard_map/layer/pallas_call | solution.py:471
  124.9 0.6 copy.17
  125.5 0.6 copy.18
  126.1 0.6 copy.19
Async XLA Ops:
  0.6 0.7 copy-start.7
  1.3 0.7 copy-start.8
  2.0 1.2 copy-start
  3.2 1.2 copy-start.1
  4.4 1.2 copy-start.2
  5.6 0.9 copy-start.3
  6.5 0.8 copy-start.4
  7.4 0.8 copy-start.5
  8.2 0.8 copy-start.6

commit v2 on v1

v2 whole, which is shorter than its diff:
```python
import functools

import jax
import jax.numpy as jnp
from jax import lax
from jax.experimental import pallas as pl
from jax.experimental.pallas import tpu as pltpu
from jax.sharding import PartitionSpec as P

MESH = pl.DeviceIdType.MESH
G = 4
CUTS = 2
F32 = jnp.float32
BF16 = jnp.bfloat16


def onehot(rows, cols, source):
    r = lax.broadcasted_iota(jnp.int32, (rows, cols), 0)
    k = lax.broadcasted_iota(jnp.int32, (rows, cols), 1)
    return jnp.where(k == source(r), 1.0, 0.0).astype(BF16)


def dot(a, b):
    return jnp.dot(a, b, preferred_element_type=F32)


def dot_t(a, b):
    return lax.dot_general(a, b, (((1,), (1,)), ((), ())), preferred_element_type=F32)


def kernel(
    nz, nh,
    span_hbm, kvw_hbm, qw_hbm, qs_hbm, ow_hbm, dec_hbm, pk_hbm, pv_hbm, ks_hbm, cl_ref,
    out_ref, nk_ref, nv_ref,
    span_ref, kvw_ref, qw_ref, qs_ref, ow_ref, dec_ref, pk_ref, pv_ref, ks_ref, in_s,
    spanbuf, wbuf, part, rsbuf, a2abuf, kvnew,
    qbuf, qrecv1, qrecv2, qrow, qup, qdn, qsc, fk, fv,
    gath, gf, lhs, obuf, orecv,
    perm_s, perm_r, w_r, up_s, dn_s,
    spc_s, spc_r, spy_s, spy_r, spf_s, spf_r,
    q1_s, q1_r, q2_s, q2_r, qu_s, qu_r, qd_s, qd_r,
    rs_s, rs_r, a2_s, a2_r, ga_s, ga_r, gy_s, gy_r, gc_s, gc_r, or_s, or_r,
):
    hpg = nh // G
    up_n, dn_n = nz // 2, nz // 2 - 1
    positions, seqs, feats = span_ref.shape
    hd = ks_ref.shape[1]
    group = qs_ref.shape[0]
    steps = dec_ref.shape[0] // seqs
    qcols = group * hd
    blk = positions * nz
    crows = kvw_ref.shape[0] // hpg
    c, h = lax.axis_index("ctx"), lax.axis_index("head")
    z, g = c // G, c % G
    yl, co = g // 2, g % 2
    core_dev = (z * G + yl * 2 + (1 - co), h)
    y_dev = (z * G + (1 - yl) * 2 + co, h)
    up_dev = (lax.rem(z + 1, nz) * G + g, h)
    dn_dev = (lax.rem(z + nz - 1, nz) * G + g, h)

    def zmod(a):
        return lax.rem(a + 2 * nz, nz)

    def rc(src, dst, ss, rs, dev):
        return pltpu.make_async_remote_copy(
            src_ref=src, dst_ref=dst, send_sem=ss, recv_sem=rs, device_id=dev, device_id_type=MESH
        )

    def other(dev):
        return jnp.logical_or(dev[0] != c, dev[1] != h)

    per = (G * nz) // nh

    def perm_to(r):
        v = yl + 2 * co
        j = v if r == 0 else nz // 2 - 1 - v
        zeta = jnp.where(lax.rem(c, per) >= G, zmod(z + j), zmod(z - j))
        return (zeta * G + h // hpg, c // per)

    def slot_of(zeta):
        away = zmod(zeta - h * per // G)
        upper = jnp.logical_and(away >= 1, away <= nz // 2)
        j = jnp.where(upper, away - 1, lax.rem(nz - away, nz))
        r = jnp.where(j >= G, 1, 0)
        v = jnp.where(j >= G, nz // 2 - 1 - j, j)
        cl = jnp.where(upper, G, 0) + lax.rem(v, 2) * 2 + v // 2
        return cl, r

    def perm_from(p):
        cl, _ = slot_of(z)
        return (h * per + cl, g * hpg + p)

    def rs_to(d):
        return (z * G + d % G, g * hpg + d // G)

    def rs_from(hs):
        return (z * G + h // hpg, hs)

    pending = []

    def finish():
        for leave in pending:
            leave()

    def sent(*copies):
        pending.extend(copy.wait_send for copy in copies)

    fetches = [
        pltpu.make_async_copy(src, dst, in_s.at[i])
        for i, (src, dst) in enumerate((
            (dec_hbm, dec_ref), (qw_hbm, qw_ref), (kvw_hbm, kvw_ref), (span_hbm, span_ref), (ks_hbm, ks_ref),
            (qs_hbm, qs_ref), (pk_hbm, pk_ref), (pv_hbm, pv_ref), (ow_hbm, ow_ref),
        ))
    ]
    for fetch in fetches:
        fetch.start()

    barrier = pltpu.get_barrier_semaphore()

    def greet(dev):
        pl.semaphore_signal(barrier, inc=1, device_id=dev, device_id_type=MESH)

    greet(core_dev)
    greet(y_dev)

    def greet_z(i, _):
        greet((zmod(z + i) * G + g, h))
        return 0

    def greet_h(i, _):
        greet((c, lax.rem(h + i, nh)))
        return 0

    lax.fori_loop(1, nz, greet_z, 0)
    lax.fori_loop(1, nh, greet_h, 0)
    for p in range(hpg):
        dev = perm_from(p)

        @pl.when(other(dev))
        def _():
            greet(dev)

    def greet_rs(hs, _):
        dev = rs_from(hs)

        @pl.when(other(dev))
        def _():
            greet(dev)

        return 0

    lax.fori_loop(0, nh, greet_rs, 0)

    for i in range(4):
        fetches[i].wait()
    order = onehot(seqs, seqs, lambda r: (r % nz) * G + r // nz)
    for p in range(positions):
        rows = dot(order, span_ref[p]).astype(BF16)
        for k in range(G):
            spanbuf[k, g, p * nz:(p + 1) * nz, :] = rows[k * nz:(k + 1) * nz]

    nrow = steps * seqs
    pick = onehot(
        nrow, nrow,
        lambda r: (r % steps) * seqs
        + ((r // steps) % nz) * G + ((r // (steps * nz)) % 2) * 2 + r // (steps * nz * 2),
    )
    decp = dot(pick, dec_ref[...]).astype(BF16)
    half = nrow // 2
    for k in range(2):
        qbuf[k, :, 0:qcols] = dot(decp[k * half:(k + 1) * half], qw_ref[...])
        qbuf[k, :, qcols:] = dot(decp[k * half:(k + 1) * half], kvw_ref[...])

    peers = 2 + (nz - 1) + (nh - 1)
    for r in range(hpg):
        peers = peers + jnp.where(other(perm_to(r)), 1, 0)
    for d in range(nh):
        peers = peers + jnp.where(other(rs_to(d)), 1, 0)
    pl.semaphore_wait(barrier, peers)

    def wrows(p, slot):
        return wbuf.at[p, pl.ds(pl.multiple_of(slot * crows, crows), crows), :]

    prows = crows // CUTS

    def wslot(m, zeta):
        cl, r = slot_of(zeta)
        start = (cl * hpg + r) * crows + (m % CUTS) * prows
        return wbuf.at[m // CUTS, pl.ds(pl.multiple_of(start, prows), prows), :]

    def perm_copy(r):
        dev = perm_to(r)
        p = h % hpg
        slot = lax.rem(c, per) * hpg + r
        return rc(kvw_hbm.at[pl.ds(r * crows, crows), :], wrows(p, slot), perm_s.at[r], perm_r.at[p], dev), dev

    for r in range(hpg):
        copy, dev = perm_copy(r)

        @pl.when(other(dev))
        def _():
            copy.start()

        @pl.when(jnp.logical_not(other(dev)))
        def _():
            wrows(h % hpg, lax.rem(c, per) * hpg + r)[...] = kvw_ref[r * crows:(r + 1) * crows, :]

    for r in range(hpg):
        def leave(r=r):
            copy, dev = perm_copy(r)
            pl.when(other(dev))(copy.wait_send)

        pending.append(leave)

    q1 = rc(qbuf.at[1 - co], qrecv1, q1_s, q1_r, core_dev)
    q1.start()
    spc = rc(spanbuf.at[:, g], spanbuf.at[:, g], spc_s, spc_r, core_dev)
    spc.start()
    q1.wait_recv()
    qh = half // 2
    for k in range(2):
        qbuf[co, k * qh:(k + 1) * qh, :] = qbuf[co, k * qh:(k + 1) * qh, :] + qrecv1[k * qh:(k + 1) * qh, :]
    q2 = rc(qbuf.at[co, pl.ds(pl.multiple_of((1 - yl) * qh, qh), qh), :], qrecv2, q2_s, q2_r, y_dev)
    q2.start()

    def spy(k):
        return rc(spanbuf.at[k, g], spanbuf.at[k, g], spy_s.at[k], spy_r.at[k], y_dev)

    def spf(k):
        gy = (1 - yl) * 2 + co
        return rc(spanbuf.at[k, gy], spanbuf.at[k, gy], spf_s.at[k], spf_r.at[k], core_dev)

    for k in range(G):
        spy(k).start()
    sent(q1, q2, spc, *[spy(k) for k in range(G)])

    def recv_w(m, zeta):
        rc(wslot(m, zeta), wslot(m, zeta), up_s.at[0, 0], w_r.at[m, zeta], up_dev).wait_recv()

    def send_up(s, m):
        zeta = zmod(z - s)
        return rc(wslot(m, zeta), wslot(m, zeta), up_s.at[s, m], w_r.at[m, zeta], up_dev)

    def send_dn(s, m):
        zeta = zmod(z + s)
        return rc(wslot(m, zeta), wslot(m, zeta), dn_s.at[s, m], w_r.at[m, zeta], dn_dev)

    def qpart(d):
        return qrow.at[pl.ds(d * steps, steps)]

    for p in range(hpg):
        cl, r = slot_of(z)
        block = wrows(p, cl * hpg + r)
        pl.when(other(perm_from(p)))(rc(block, block, perm_s.at[0], perm_r.at[p], up_dev).wait_recv)
        for m in range(p * CUTS, (p + 1) * CUTS):
            send_up(0, m).start()
            send_dn(0, m).start()

    q2.wait_recv()
    own = qbuf[co, pl.ds(pl.multiple_of(yl * qh, qh), qh), :] + qrecv2[...]
    for r in range(qh):
        qrow[r, 0:1, :] = own[r:r + 1, :]

    def q_up(s):
        src = qpart(zmod(z + up_n)) if s == 0 else qup.at[s - 1]
        return rc(src, qup.at[s], qu_s.at[s], qu_r.at[s], up_dev)

    def q_dn(s):
        src = qpart(zmod(z - dn_n)) if s == 0 else qdn.at[s - 1]
        return rc(src, qdn.at[s], qd_s.at[s], qd_r.at[s], dn_dev)

    q_up(0).start()
    q_dn(0).start()
    parts = hpg * CUTS
    for s in range(1, up_n):
        for m in range(parts):
            recv_w(m, zmod(z - s))
            send_up(s, m).start()
            if s <= dn_n:
                recv_w(m, zmod(z + s))
            if s < dn_n:
                send_dn(s, m).start()
            if m == parts // 2 - 1:
                q_up(s - 1).wait_recv()
                qup[s - 1] = qup[s - 1] + qpart(zmod(z + up_n - s))[...]
                q_up(s).start()
                if s < dn_n:
                    q_dn(s - 1).wait_recv()
                    qdn[s - 1] = qdn[s - 1] + qpart(zmod(z - dn_n + s))[...]
                    q_dn(s).start()
        k = s - up_n + G
        if k >= 0:
            spy(k).wait_recv()
            spf(k).start()
    for m in range(parts):
        recv_w(m, zmod(z - up_n))
    spc.wait_recv()
    for k in range(G):
        spf(k).wait_recv()

    sent(*[spf(k) for k in range(G)])
    for s in range(up_n):
        sent(*[send_up(s, m) for m in range(parts)], q_up(s))
        if s < dn_n:
            sent(*[send_dn(s, m) for m in range(parts)], q_dn(s))

    def rs_copy(d, kind):
        return rc(part.at[d, kind], rsbuf.at[h, kind], rs_s.at[d, kind], rs_r.at[h, kind], rs_to(d))

    def product(i, _):
        d = lax.rem(i + h, nh)
        tile = spanbuf[d % G].reshape(G * blk, feats)
        sums = dot(tile, wbuf[d // G]).astype(BF16)
        part[d, 0] = sums[:, :hd]
        part[d, 1] = sums[:, hd:]
        away = other(rs_to(d))

        @pl.when(away)
        def _():
            rs_copy(d, 0).start()

        @pl.when(jnp.logical_not(away))
        def _():
            rsbuf[h] = part[d]

        return 0

    lax.fori_loop(0, nh, product, 0)

    def send_values(i, _):
        d = lax.rem(i + h, nh)
        pl.when(other(rs_to(d)))(lambda: rs_copy(d, 1).start())
        return 0

    lax.fori_loop(0, nh, send_values, 0)

    def rs_done(d, _):
        @pl.when(other(rs_to(d)))
        def _():
            rs_copy(d, 0).wait_send()
            rs_copy(d, 1).wait_send()

        return 0

    pending.append(lambda: lax.fori_loop(0, nh, rs_done, 0))

    q_up(up_n - 1).wait_recv()
    q_dn(dn_n - 1).wait_recv()
    qv = qpart(z)[...] + qup[up_n - 1] + qdn[dn_n - 1]
    for i in range(4, len(fetches)):
        fetches[i].wait()
    ks = ks_ref[...]
    fk[...] = jnp.zeros_like(fk)
    fv[...] = jnp.zeros_like(fv)
    for t in range(steps):
        for j in range(group):
            qsc[t * group + j:t * group + j + 1, :] = qv[t, 0:1, j * hd:(j + 1) * hd]
        fk[t:t + 1, :] = qv[t, 0:1, qcols:qcols + hd] / ks
        fv[t:t + 1, :] = qv[t, 0:1, qcols + hd:qcols + 2 * hd]
    scale = jnp.concatenate([qs_ref[...]] * steps, 0)
    scaled = (qsc[...] * scale * ks * (hd ** -0.5)).astype(BF16)
    s_old = dot_t(scaled, pk_ref[...])
    where = lax.broadcasted_iota(jnp.int32, s_old.shape, 1)
    s_old = jnp.where(where < cl_ref[0], s_old, -1e30)
    s_fresh = dot_t(scaled, fk[...].astype(BF16))
    col = lax.broadcasted_iota(jnp.int32, s_fresh.shape, 1)
    row = lax.broadcasted_iota(jnp.int32, s_fresh.shape, 0)
    s_fresh = jnp.where(col <= row // group, s_fresh, -1e30)
    top0 = jnp.maximum(jnp.max(s_old, 1, keepdims=True), jnp.max(s_fresh, 1, keepdims=True))

    pos = G * positions
    spread = onehot(G * blk, G * blk, lambda r: (r % pos) * nz + r // pos)

    def a2_copy(i, kind):
        zt = zmod(z + i)
        return rc(a2abuf.at[kind, zt], kvnew.at[kind, z], a2_s.at[kind, i], a2_r.at[kind, z], (zt * G + g, h))

    def a2_done(i, _):
        a2_copy(i, 0).wait_send()
        a2_copy(i, 1).wait_send()
        return 0

    for kind in range(2):
        for hs in range(nh):
            slot = rsbuf.at[hs, kind]
            pl.when(other(rs_from(hs)))(rc(slot, slot, rs_s.at[0, 0], rs_r.at[hs, kind], core_dev).wait_recv)
        sums = rsbuf[0, kind].astype(F32)
        for hs in range(1, nh):
            sums = sums + rsbuf[hs, kind].astype(F32)
        if kind == 0:
            sums = sums / ks
        a2abuf[kind] = dot(spread, sums.astype(BF16)).astype(BF16).reshape(nz, pos, hd)

        def a2_start(i, _, kind=kind):
            a2_copy(i, kind).start()
            return 0

        lax.fori_loop(1, nz, a2_start, 0)
        kvnew[kind, z] = a2abuf[kind, z]

    pending.append(lambda: lax.fori_loop(1, nz, a2_done, 0))

    def arrived(kind):
        def a2_wait(i, _):
            zt = zmod(z + i)
            slot = kvnew.at[kind, zt]
            rc(slot, slot, a2_s.at[0, 0], a2_r.at[kind, zt], core_dev).wait_recv()
            return 0

        lax.fori_loop(1, nz, a2_wait, 0)
        return kvnew[kind].reshape(nz * pos, hd)

    k_new = arrived(0)
    nk_ref[...] = k_new
    s_new = dot_t(scaled, k_new)
    top = jnp.maximum(top0, jnp.max(s_new, 1, keepdims=True))
    w_old, w_new, w_fresh = jnp.exp(s_old - top), jnp.exp(s_new - top), jnp.exp(s_fresh - top)
    total = (
        jnp.sum(w_old, 1, keepdims=True) + jnp.sum(w_new, 1, keepdims=True) + jnp.sum(w_fresh, 1, keepdims=True)
    )
    mixed = dot(w_old.astype(BF16), pv_ref[...]) + dot(w_fresh.astype(BF16), fv[...].astype(BF16))
    v_new = arrived(1)
    nv_ref[...] = v_new
    mixed = (mixed + dot(w_new.astype(BF16), v_new)) / total
    gath[z, g] = mixed.astype(BF16)

    gy_of = (1 - yl) * 2 + co

    def zig(i):
        return zmod(z + jnp.where(lax.rem(i, 2) == 1, (i + 1) // 2, -(i // 2)))

    def ga_copy(i):
        return rc(gath.at[z, g], gath.at[z, g], ga_s.at[i], ga_r.at[z], (zig(i) * G + g, h))

    def gy_copy(zt):
        return rc(gath.at[zt, g], gath.at[zt, g], gy_s.at[zt], gy_r.at[zt], y_dev)

    def gc_copy(zt, k):
        gk = g if k == 0 else gy_of
        return rc(gath.at[zt, gk], gath.at[zt, gk], gc_s.at[k, zt], gc_r.at[k, zt], core_dev)

    def ga_start(i, _):
        ga_copy(i).start()
        return 0

    lax.fori_loop(1, nz, ga_start, 0)
    gy_copy(z).start()
    gc_copy(z, 0).start()

    def hand_on(i, _):
        zt = zig(i)
        rc(gath.at[zt, g], gath.at[zt, g], ga_s.at[0], ga_r.at[zt], core_dev).wait_recv()
        gy_copy(zt).start()
        gc_copy(zt, 0).start()
        return 0

    def hand_over(i, _):
        zt = zig(i)
        rc(gath.at[zt, gy_of], gath.at[zt, gy_of], ga_s.at[0], gy_r.at[zt], core_dev).wait_recv()
        gc_copy(zt, 1).start()
        return 0

    def gc_wait(zt, _):
        for k in range(2):
            slot = gath.at[zt, (yl if k == 0 else 1 - yl) * 2 + 1 - co]
            rc(slot, slot, ga_s.at[0], gc_r.at[k, zt], core_dev).wait_recv()
        return 0

    lax.fori_loop(1, nz, hand_on, 0)
    lax.fori_loop(0, nz, hand_over, 0)
    lax.fori_loop(0, nz, gc_wait, 0)

    def ga_done(i, _):
        pl.when(i > 0)(lambda: ga_copy(i).wait_send())
        gy_copy(i).wait_send()
        gc_copy(i, 0).wait_send()
        gc_copy(i, 1).wait_send()
        return 0

    pending.append(lambda: lax.fori_loop(0, nz, ga_done, 0))

    gf[...] = gath[...].reshape(gf.shape).astype(F32)
    for t in range(steps):
        for j in range(group):
            rows = gf[pl.ds(t * group + j, seqs, stride=steps * group), :]
            lhs[t * seqs:(t + 1) * seqs, j * hd:(j + 1) * hd] = rows.astype(BF16)
    obuf[...] = dot(lhs[...], ow_ref[...]).reshape(obuf.shape)
    mine = seqs // nh

    def or_copy(i):
        ht = lax.rem(h + i, nh)
        src = obuf.at[:, pl.ds(pl.multiple_of(ht * mine, mine), mine), :]
        return rc(src, orecv.at[h], or_s.at[i], or_r.at[h], (c, ht))

    def or_start(i, _):
        or_copy(i).start()
        return 0

    lax.fori_loop(1, nh, or_start, 0)
    orecv[h] = obuf[:, pl.ds(pl.multiple_of(h * mine, mine), mine), :]

    def or_wait(i, _):
        hs = lax.rem(h + i, nh)
        rc(orecv.at[hs], orecv.at[hs], or_s.at[0], or_r.at[hs], core_dev).wait_recv()
        return 0

    lax.fori_loop(1, nh, or_wait, 0)
    def or_done(i, _):
        or_copy(i).wait_send()
        return 0

    pending.append(lambda: lax.fori_loop(1, nh, or_done, 0))
    result = orecv[0]
    for hs in range(1, nh):
        result = result + orecv[hs]
    out_ref[...] = result.astype(BF16)

    finish()


def body(
    span_states, kv_weight, q_weight, q_scale, out_weight, decode_states, prior_keys, prior_values, key_scale, cached_len
):
    nh = lax.axis_size("head")
    nz = lax.axis_size("ctx") // G
    hpg = nh // G
    positions, seqs, feats = span_states.shape
    hd = key_scale.shape[0]
    qcols = q_scale.shape[0]
    group = qcols // hd
    steps, _, depth = decode_states.shape
    width = qcols + 2 * hd
    nrow = steps * seqs
    blk = positions * nz
    pos = G * positions
    ocols = out_weight.shape[1]
    prior = prior_keys.shape[1]
    vm = pltpu.VMEM
    dma = pltpu.SemaphoreType.DMA
    up_n, dn_n = nz // 2, nz // 2 - 1
    vspec = pl.BlockSpec(memory_space=pltpu.VMEM)
    operands = (
        span_states, kv_weight, q_weight, q_scale.reshape(group, hd), out_weight,
        decode_states.reshape(nrow, depth), prior_keys.reshape(prior, hd), prior_values.reshape(prior, hd),
        key_scale.reshape(1, hd),
    )
    out, nk, nv = pl.pallas_call(
        functools.partial(kernel, nz, nh),
        out_shape=(
            jax.ShapeDtypeStruct((steps, seqs // nh, ocols), BF16),
            jax.ShapeDtypeStruct((nz * pos, hd), BF16),
            jax.ShapeDtypeStruct((nz * pos, hd), BF16),
        ),
        in_specs=[pl.BlockSpec(memory_space=pl.ANY)] * 9 + [pl.BlockSpec(memory_space=pltpu.SMEM)],
        out_specs=(vspec,) * 3,
        scratch_shapes=[
            *[vm(a.shape, a.dtype) for a in operands], dma((len(operands),)),
            vm((G, G, blk, feats), BF16),
            vm((hpg, feats, 2 * hd), BF16),
            vm((nh, 2, G * blk, hd), BF16),
            vm((nh, 2, G * blk, hd), BF16),
            vm((2, nz, pos, hd), BF16),
            vm((2, nz, pos, hd), BF16),
            vm((2, nrow // 2, width), F32),
            vm((nrow // 2, width), F32),
            vm((nrow // 4, width), F32),
            vm((nrow // 4, 1, width), F32),
            vm((up_n, steps, 1, width), F32),
            vm((dn_n, steps, 1, width), F32),
            vm((steps * group, hd), F32),
            vm((16, hd), F32),
            vm((16, hd), F32),
            vm((nz, G, steps * group, hd), BF16),
            vm((seqs * steps * group, hd), F32),
            vm((nrow, qcols), BF16),
            vm((steps, seqs, ocols), F32),
            vm((nh, steps, seqs // nh, ocols), F32),
            dma((hpg,)), dma((hpg,)), dma((hpg * CUTS, nz)), dma((up_n, hpg * CUTS)), dma((dn_n, hpg * CUTS)),
            dma, dma, dma((G,)), dma((G,)), dma((G,)), dma((G,)),
            dma, dma, dma, dma, dma((up_n,)), dma((up_n,)), dma((dn_n,)), dma((dn_n,)),
            dma((nh, 2)), dma((nh, 2)), dma((2, nz)), dma((2, nz)), dma((nz,)), dma((nz,)),
            dma((nz,)), dma((nz,)), dma((2, nz)), dma((2, nz)), dma((nh,)), dma((nh,)),
        ],
        compiler_params=pltpu.CompilerParams(
            collective_id=0, has_side_effects=True, vmem_limit_bytes=60 * 2**20
        ),
        name="layer",
    )(*operands, cached_len)
    return out, nk.reshape(1, nz * pos, hd), nv.reshape(1, nz * pos, hd)


def solution(mesh):
    return jax.shard_map(
        body,
        mesh=mesh,
        in_specs=(
            P("ctx", None, "head"),
            P("ctx", "head"),
            P("ctx", "head"),
            P("head"),
            P("head", "ctx"),
            P(None, None, "ctx"),
            P("ctx", None, "head"),
            P("ctx", None, "head"),
            P("head"),
            P("ctx"),
        ),
        out_specs=(P(None, "head", "ctx"), P("ctx", None, "head"), P("ctx", None, "head")),
        check_vma=False,
    )
```

time: 127 us -> 114 us (0.90)
  Pallas kernels: 116 us -> 109 us
  local copies, waits for them, and re-layouts: 9.6 us -> 3.43 us
    pallas_call x1, Pallas kernels: 116 us -> 109 us  [body(): pl.pallas_call(functools.partial(kernel, nz, nh), out_shape=(jax.ShapeDty...]
    unnamed x21 -> x7, local copies, waits for them, and re-layouts: 9.6 us -> 3.43 us
where the time goes in v2:
time: 114 us
  Pallas kernels  109 us (96%)
  local copies, waits for them, and re-layouts  3.43 us (3%)
  between operations  1.3 us (1%)
    pallas_call x1, Pallas kernels, body(): pl.pallas_call(functools.partial(kernel, nz, nh), out_shape=(jax.ShapeDty...  109 us
    unnamed x7, local copies, waits for them, and re-layouts  3.43 us

profile of v2, /device:TPU:1, one launch (start us, length us, event | category | flops | bytes accessed | tf_op | source)
XLA Modules:
  0.0 114.1 jit_solution(2729555900958843159)
XLA Ops:
  1.3 109.4 %layer.1 = (bf16[2,8,256]{2,1,0:T(8,128)(2,1)}, bf16[256,128]{1,0:T(8,128)(2,1)}, bf16[256,128]{1,0:T(8,128)(2,1)}) custom-call(bf16[4,64,2048]{2,1,0:T(8,128)(2,1)} %span_hbm.1, bf16[256,256]{1,0:T(8,128)(2,1)} %kvw_hbm.1, bf16[256,2048]{1,0:T(8,128)(2,1)} %qw_hbm.1, f32[16,128]{1,0:T(8,128)} %bitcast.12, bf16[2048,256]{1,0:T(8,128)(2,1)} %ow_hbm.1, ...), custom_call_target="tpu_custom_call" | custom-call | tf_op jit(solution)/shard_map/layer/pallas_call | solution.py:547
  110.7 0.0 copy-start.1
  110.7 0.7 copy-done.1
  111.4 0.6 copy.17
  112.0 0.0 copy-start
  112.0 1.5 %copy.18 = bf16[1,256,128]{2,1,0:T(8,128)(2,1)} copy(bf16[1,256,128]{2,1,0:T(8,128)(2,1)} %bitcast.11) | data formatting | bytes 131072
  113.5 0.0 copy-done
  113.5 0.6 copy.19
Async XLA Ops:
  110.7 0.7 copy-start.1
  112.0 1.5 %copy-start = (bf16[256,128]{1,0:T(8,128)(2,1)S(1)}, bf16[256,128]{1,0:T(8,128)(2,1)}, u32[]{:S(2)}) copy-start(bf16[256,128]{1,0:T(8,128)(2,1)} %get-tuple-element.8) | copy-start | bytes 196612

commit v3 on v2

--- a/solution.py
+++ b/solution.py
@@ -30,9 +30,9 @@
 
 def kernel(
     nz, nh,
-    span_hbm, kvw_hbm, qw_hbm, qs_hbm, ow_hbm, dec_hbm, pk_hbm, pv_hbm, ks_hbm, cl_ref,
-    out_ref, nk_ref, nv_ref,
-    span_ref, kvw_ref, qw_ref, qs_ref, ow_ref, dec_ref, pk_ref, pv_ref, ks_ref, in_s,
+    span_hbm, kvw_hbm, qw_hbm, qs_hbm, ow_hbm, dec_hbm, pk_hbm, pv_hbm, ks_hbm, cl_hbm,
+    out_ref, kv_ref,
+    span_ref, kvw_ref, qw_ref, qs_ref, ow_ref, dec_ref, pk_ref, pv_ref, ks_ref, cl_ref, in_s,
     spanbuf, wbuf, part, rsbuf, a2abuf, kvnew,
     qbuf, qrecv1, qrecv2, qrow, qup, qdn, qsc, fk, fv,
     gath, gf, lhs, obuf, orecv,
@@ -69,13 +69,20 @@
     def other(dev):
         return jnp.logical_or(dev[0] != c, dev[1] != h)
 
+    def group_of(head):
+        pair = head // hpg
+        return (pair // 2 + pair % 2) % 2 * 2 + pair % 2
+
+    def heads_of(p):
+        return ((co + yl) % 2 * 2 + co) * hpg + p
+
     per = (G * nz) // nh
 
     def perm_to(r):
         v = yl + 2 * co
         j = v if r == 0 else nz // 2 - 1 - v
         zeta = jnp.where(lax.rem(c, per) >= G, zmod(z + j), zmod(z - j))
-        return (zeta * G + h // hpg, c // per)
+        return (zeta * G + group_of(h), c // per)
 
     def slot_of(zeta):
         away = zmod(zeta - h * per // G)
@@ -88,13 +95,13 @@
 
     def perm_from(p):
         cl, _ = slot_of(z)
-        return (h * per + cl, g * hpg + p)
+        return (h * per + cl, heads_of(p))
 
     def rs_to(d):
-        return (z * G + d % G, g * hpg + d // G)
+        return (z * G + d % G, heads_of(d // G))
 
     def rs_from(hs):
-        return (z * G + h // hpg, hs)
+        return (z * G + group_of(h), hs)
 
     pending = []
 
@@ -109,7 +116,7 @@
         pltpu.make_async_copy(src, dst, in_s.at[i])
         for i, (src, dst) in enumerate((
             (dec_hbm, dec_ref), (qw_hbm, qw_ref), (kvw_hbm, kvw_ref), (span_hbm, span_ref), (ks_hbm, ks_ref),
-            (qs_hbm, qs_ref), (pk_hbm, pk_ref), (pv_hbm, pv_ref), (ow_hbm, ow_ref),
+            (qs_hbm, qs_ref), (pk_hbm, pk_ref), (pv_hbm, pv_ref), (ow_hbm, ow_ref), (cl_hbm, cl_ref),
         ))
     ]
     for fetch in fetches:
@@ -150,6 +157,50 @@
         return 0
 
     lax.fori_loop(0, nh, greet_rs, 0)
+
+    peers = 2 + (nz - 1) + (nh - 1)
+    for r in range(hpg):
+        peers = peers + jnp.where(other(perm_to(r)), 1, 0)
+    for d in range(nh):
+        peers = peers + jnp.where(other(rs_to(d)), 1, 0)
+    pl.semaphore_wait(barrier, peers)
+
+    def wrows(p, slot):
+        return wbuf.at[p, pl.ds(pl.multiple_of(slot * crows, crows), crows), :]
+
+    prows = crows // CUTS
+
+    def wslot(m, zeta):
+        cl, r = slot_of(zeta)
+        start = (cl * hpg + r) * crows + (m % CUTS) * prows
+        return wbuf.at[m // CUTS, pl.ds(pl.multiple_of(start, prows), prows), :]
+
+    def perm_copy(r):
+        dev = perm_to(r)
+        p = h % hpg
+        slot = lax.rem(c, per) * hpg + r
+        return rc(kvw_hbm.at[pl.ds(r * crows, crows), :], wrows(p, slot), perm_s.at[r], perm_r.at[p], dev), dev
+
+    for r in range(hpg):
+        copy, dev = perm_copy(r)
+
+        @pl.when(other(dev))
+        def _():
+            copy.start()
+
+        @pl.when(jnp.logical_not(other(dev)))
+        def _():
+            here = wrows(h % hpg, lax.rem(c, per) * hpg + r)
+            own_block = pltpu.make_async_copy(kvw_hbm.at[pl.ds(r * crows, crows), :], here, perm_s.at[r])
+            own_block.start()
+            own_block.wait()
+
+    for r in range(hpg):
+        def leave(r=r):
+            copy, dev = perm_copy(r)
+            pl.when(other(dev))(copy.wait_send)
+
+        pending.append(leave)
 
     for i in range(4):
         fetches[i].wait()
@@ -171,47 +222,6 @@
         qbuf[k, :, 0:qcols] = dot(decp[k * half:(k + 1) * half], qw_ref[...])
         qbuf[k, :, qcols:] = dot(decp[k * half:(k + 1) * half], kvw_ref[...])
 
-    peers = 2 + (nz - 1) + (nh - 1)
-    for r in range(hpg):
-        peers = peers + jnp.where(other(perm_to(r)), 1, 0)
-    for d in range(nh):
-        peers = peers + jnp.where(other(rs_to(d)), 1, 0)
-    pl.semaphore_wait(barrier, peers)
-
-    def wrows(p, slot):
-        return wbuf.at[p, pl.ds(pl.multiple_of(slot * crows, crows), crows), :]
-
-    prows = crows // CUTS
-
-    def wslot(m, zeta):
-        cl, r = slot_of(zeta)
-        start = (cl * hpg + r) * crows + (m % CUTS) * prows
-        return wbuf.at[m // CUTS, pl.ds(pl.multiple_of(start, prows), prows), :]
-
-    def perm_copy(r):
-        dev = perm_to(r)
-        p = h % hpg
-        slot = lax.rem(c, per) * hpg + r
-        return rc(kvw_hbm.at[pl.ds(r * crows, crows), :], wrows(p, slot), perm_s.at[r], perm_r.at[p], dev), dev
-
-    for r in range(hpg):
-        copy, dev = perm_copy(r)
-
-        @pl.when(other(dev))
-        def _():
-            copy.start()
-
-        @pl.when(jnp.logical_not(other(dev)))
-        def _():
-            wrows(h % hpg, lax.rem(c, per) * hpg + r)[...] = kvw_ref[r * crows:(r + 1) * crows, :]
-
-    for r in range(hpg):
-        def leave(r=r):
-            copy, dev = perm_copy(r)
-            pl.when(other(dev))(copy.wait_send)
-
-        pending.append(leave)
-
     q1 = rc(qbuf.at[1 - co], qrecv1, q1_s, q1_r, core_dev)
     q1.start()
     spc = rc(spanbuf.at[:, g], spanbuf.at[:, g], spc_s, spc_r, core_dev)
@@ -256,11 +266,6 @@
             send_up(0, m).start()
             send_dn(0, m).start()
 
-    q2.wait_recv()
-    own = qbuf[co, pl.ds(pl.multiple_of(yl * qh, qh), qh), :] + qrecv2[...]
-    for r in range(qh):
-        qrow[r, 0:1, :] = own[r:r + 1, :]
-
     def q_up(s):
         src = qpart(zmod(z + up_n)) if s == 0 else qup.at[s - 1]
         return rc(src, qup.at[s], qu_s.at[s], qu_r.at[s], up_dev)
@@ -269,29 +274,45 @@
         src = qpart(zmod(z - dn_n)) if s == 0 else qdn.at[s - 1]
         return rc(src, qdn.at[s], qd_s.at[s], qd_r.at[s], dn_dev)
 
-    q_up(0).start()
-    q_dn(0).start()
+    def q_step(s):
+        if s == 0:
+            q2.wait_recv()
+            own = qbuf[co, pl.ds(pl.multiple_of(yl * qh, qh), qh), :] + qrecv2[...]
+            for r in range(qh):
+                qrow[r, 0:1, :] = own[r:r + 1, :]
+        else:
+            q_up(s - 1).wait_recv()
+            qup[s - 1] = qup[s - 1] + qpart(zmod(z + up_n - s))[...]
+        q_up(s).start()
+        if s < dn_n:
+            if s > 0:
+                q_dn(s - 1).wait_recv()
+                qdn[s - 1] = qdn[s - 1] + qpart(zmod(z - dn_n + s))[...]
+            q_dn(s).start()
+
     parts = hpg * CUTS
+
+    def goes_up(s, m):
+        return s < up_n - 1 or m < parts // 2
+
+    def goes_dn(s, m):
+        return s < up_n - 1 or m >= parts // 2
+
     for s in range(1, up_n):
         for m in range(parts):
             recv_w(m, zmod(z - s))
-            send_up(s, m).start()
-            if s <= dn_n:
-                recv_w(m, zmod(z + s))
-            if s < dn_n:
+            if goes_up(s, m):
+                send_up(s, m).start()
+            recv_w(m, zmod(z + s))
+            if goes_dn(s, m):
                 send_dn(s, m).start()
-            if m == parts // 2 - 1:
-                q_up(s - 1).wait_recv()
-                qup[s - 1] = qup[s - 1] + qpart(zmod(z + up_n - s))[...]
-                q_up(s).start()
-                if s < dn_n:
-                    q_dn(s - 1).wait_recv()
-                    qdn[s - 1] = qdn[s - 1] + qpart(zmod(z - dn_n + s))[...]
-                    q_dn(s).start()
+            if m == parts // 2 - 1 and s >= 2:
+                q_step(s - 2)
         k = s - up_n + G
         if k >= 0:
             spy(k).wait_recv()
             spf(k).start()
+    q_step(up_n - 2)
     for m in range(parts):
         recv_w(m, zmod(z - up_n))
     spc.wait_recv()
@@ -300,9 +321,10 @@
 
     sent(*[spf(k) for k in range(G)])
     for s in range(up_n):
-        sent(*[send_up(s, m) for m in range(parts)], q_up(s))
+        sent(*[send_up(s, m) for m in range(parts) if goes_up(s, m)], q_up(s))
+        sent(*[send_dn(s, m) for m in range(parts) if goes_dn(s, m)])
         if s < dn_n:
-            sent(*[send_dn(s, m) for m in range(parts)], q_dn(s))
+            sent(q_dn(s))
 
     def rs_copy(d, kind):
         return rc(part.at[d, kind], rsbuf.at[h, kind], rs_s.at[d, kind], rs_r.at[h, kind], rs_to(d))
@@ -344,6 +366,7 @@
 
     pending.append(lambda: lax.fori_loop(0, nh, rs_done, 0))
 
+    q_step(up_n - 1)
     q_up(up_n - 1).wait_recv()
     q_dn(dn_n - 1).wait_recv()
     qv = qpart(z)[...] + qup[up_n - 1] + qdn[dn_n - 1]
@@ -371,8 +394,11 @@
     pos = G * positions
     spread = onehot(G * blk, G * blk, lambda r: (r % pos) * nz + r // pos)
 
+    def zig(i):
+        return zmod(z + jnp.where(lax.rem(i, 2) == 1, (i + 1) // 2, -(i // 2)))
+
     def a2_copy(i, kind):
-        zt = zmod(z + i)
+        zt = zig(nz - i)
         return rc(a2abuf.at[kind, zt], kvnew.at[kind, z], a2_s.at[kind, i], a2_r.at[kind, z], (zt * G + g, h))
 
     def a2_done(i, _):
@@ -402,7 +428,7 @@
 
     def arrived(kind):
         def a2_wait(i, _):
-            zt = zmod(z + i)
+            zt = zig(i)
             slot = kvnew.at[kind, zt]
             rc(slot, slot, a2_s.at[0, 0], a2_r.at[kind, zt], core_dev).wait_recv()
             return 0
@@ -411,7 +437,6 @@
         return kvnew[kind].reshape(nz * pos, hd)
 
     k_new = arrived(0)
-    nk_ref[...] = k_new
     s_new = dot_t(scaled, k_new)
     top = jnp.maximum(top0, jnp.max(s_new, 1, keepdims=True))
     w_old, w_new, w_fresh = jnp.exp(s_old - top), jnp.exp(s_new - top), jnp.exp(s_fresh - top)
@@ -420,17 +445,14 @@
     )
     mixed = dot(w_old.astype(BF16), pv_ref[...]) + dot(w_fresh.astype(BF16), fv[...].astype(BF16))
     v_new = arrived(1)
-    nv_ref[...] = v_new
+    kv_ref[...] = kvnew[...].reshape(kv_ref.shape)
     mixed = (mixed + dot(w_new.astype(BF16), v_new)) / total
     gath[z, g] = mixed.astype(BF16)
 
     gy_of = (1 - yl) * 2 + co
 
-    def zig(i):
-        return zmod(z + jnp.where(lax.rem(i, 2) == 1, (i + 1) // 2, -(i // 2)))
-
     def ga_copy(i):
-        return rc(gath.at[z, g], gath.at[z, g], ga_s.at[i], ga_r.at[z], (zig(i) * G + g, h))
+        return rc(gath.at[z, g], gath.at[z, g], ga_s.at[i], ga_r.at[z], (zig(nz - i) * G + g, h))
 
     def gy_copy(zt):
         return rc(gath.at[zt, g], gath.at[zt, g], gy_s.at[zt], gy_r.at[zt], y_dev)
@@ -516,6 +538,17 @@
     out_ref[...] = result.astype(BF16)
 
     finish()
+
+
+def place(out_ref, kv_ref, attn_ref, nk_ref, nv_ref, sems):
+    moves = [
+        pltpu.make_async_copy(src, dst, sems.at[i])
+        for i, (src, dst) in enumerate(((kv_ref.at[0], nk_ref.at[0]), (kv_ref.at[1], nv_ref.at[0]), (out_ref, attn_ref)))
+    ]
+    for move in moves:
+        move.start()
+    for move in moves:
+        move.wait()
 
 
 def body(
@@ -544,17 +577,16 @@
         decode_states.reshape(nrow, depth), prior_keys.reshape(prior, hd), prior_values.reshape(prior, hd),
         key_scale.reshape(1, hd),
     )
-    out, nk, nv = pl.pallas_call(
+    out, kv = pl.pallas_call(
         functools.partial(kernel, nz, nh),
         out_shape=(
             jax.ShapeDtypeStruct((steps, seqs // nh, ocols), BF16),
-            jax.ShapeDtypeStruct((nz * pos, hd), BF16),
-            jax.ShapeDtypeStruct((nz * pos, hd), BF16),
+            jax.ShapeDtypeStruct((2, nz * pos, hd), BF16),
         ),
-        in_specs=[pl.BlockSpec(memory_space=pl.ANY)] * 9 + [pl.BlockSpec(memory_space=pltpu.SMEM)],
-        out_specs=(vspec,) * 3,
+        in_specs=[pl.BlockSpec(memory_space=pl.ANY)] * 10,
+        out_specs=(vspec,) * 2,
         scratch_shapes=[
-            *[vm(a.shape, a.dtype) for a in operands], dma((len(operands),)),
+            *[vm(a.shape, a.dtype) for a in operands], pltpu.SMEM((1,), jnp.int32), dma((len(operands) + 1,)),
             vm((G, G, blk, feats), BF16),
             vm((hpg, feats, 2 * hd), BF16),
             vm((nh, 2, G * blk, hd), BF16),
@@ -575,7 +607,7 @@
             vm((nrow, qcols), BF16),
             vm((steps, seqs, ocols), F32),
             vm((nh, steps, seqs // nh, ocols), F32),
-            dma((hpg,)), dma((hpg,)), dma((hpg * CUTS, nz)), dma((up_n, hpg * CUTS)), dma((dn_n, hpg * CUTS)),
+            dma((hpg,)), dma((hpg,)), dma((hpg * CUTS, nz)), dma((up_n, hpg * CUTS)), dma((up_n, hpg * CUTS)),
             dma, dma, dma((G,)), dma((G,)), dma((G,)), dma((G,)),
             dma, dma, dma, dma, dma((up_n,)), dma((up_n,)), dma((dn_n,)), dma((dn_n,)),
             dma((nh, 2)), dma((nh, 2)), dma((2, nz)), dma((2, nz)), dma((nz,)), dma((nz,)),
@@ -586,7 +618,19 @@
         ),
         name="layer",
     )(*operands, cached_len)
-    return out, nk.reshape(1, nz * pos, hd), nv.reshape(1, nz * pos, hd)
+    return pl.pallas_call(
+        place,
+        out_shape=(
+            jax.ShapeDtypeStruct(out.shape, BF16),
+            jax.ShapeDtypeStruct((1, nz * pos, hd), BF16),
+            jax.ShapeDtypeStruct((1, nz * pos, hd), BF16),
+        ),
+        in_specs=[pl.BlockSpec(memory_space=pl.ANY)] * 2,
+        out_specs=(pl.BlockSpec(memory_space=pl.ANY),) * 3,
+        scratch_shapes=[dma((3,))],
+        compiler_params=pltpu.CompilerParams(vmem_limit_bytes=60 * 2**20),
+        name="place",
+    )(out, kv)
 
 
 def solution(mesh):

time: 114 us -> 113 us (level)
  local copies, waits for them, and re-layouts: 3.43 us -> 0 us
  Pallas kernels: 109 us -> 112 us
    pallas_call x0 -> x1, Pallas kernels: none -> 5.35 us  [body(): pl.pallas_call(place, out_shape=(jax.ShapeDtypeStruct(out.shape, BF16), j...]
    unnamed x7 -> x0, local copies, waits for them, and re-layouts: 3.43 us -> none
    pallas_call x1, Pallas kernels: 109 us -> 107 us  [body(): pl.pallas_call(functools.partial(kernel, nz, nh), out_shape=(jax.ShapeDty...]
where the time goes in v3:
time: 113 us
  Pallas kernels  112 us (99%)
  between operations  1.29 us (1%)
    pallas_call x1, Pallas kernels, body(): pl.pallas_call(functools.partial(kernel, nz, nh), out_shape=(jax.ShapeDty...  107 us
    pallas_call x1, Pallas kernels, body(): pl.pallas_call(place, out_shape=(jax.ShapeDtypeStruct(out.shape, BF16), j...  5.35 us

profile of v3, /device:TPU:1, one launch (start us, length us, event | category | flops | bytes accessed | tf_op | source)
XLA Modules:
  0.0 113.2 jit_solution(2041197918486085402)
XLA Ops:
  1.3 106.5 %layer.1 = (bf16[2,8,256]{2,1,0:T(8,128)(2,1)}, bf16[2,256,128]{2,1,0:T(8,128)(2,1)}) custom-call(bf16[4,64,2048]{2,1,0:T(8,128)(2,1)} %span_hbm.1, bf16[256,256]{1,0:T(8,128)(2,1)} %kvw_hbm.1, bf16[256,2048]{1,0:T(8,128)(2,1)} %qw_hbm.1, f32[16,128]{1,0:T(8,128)} %bitcast.8, bf16[2048,256]{1,0:T(8,128)(2,1)} %ow_hbm.1, bf16[128,256]{1,0:T(8,128)(2,1)} %bitcast.5, ...), custom_call_target="tpu_custom_call" | custom-call | tf_op jit(solution)/shard_map/layer/pallas_call | solution.py:580
  107.8 5.3 %place.1 = (bf16[2,8,256]{2,1,0:T(8,128)(2,1)}, bf16[1,256,128]{2,1,0:T(8,128)(2,1)}, bf16[1,256,128]{2,1,0:T(8,128)(2,1)}) custom-call(bf16[2,8,256]{2,1,0:T(8,128)(2,1)} %get-tuple-element.5.out_ref, bf16[2,256,128]{2,1,0:T(8,128)(2,1)} %get-tuple-element.6.kv_ref), custom_call_target="tpu_custom_call" | custom-call | tf_op jit(solution)/shard_map/place/pallas_call | solution.py:621

commit v4 on v3

--- a/solution.py
+++ b/solution.py
@@ -394,6 +394,12 @@
     pos = G * positions
     spread = onehot(G * blk, G * blk, lambda r: (r % pos) * nz + r // pos)
 
+    def slot_at(zr, zs):
+        return zmod(zs - (zr - zr % 2) + nz // 2)
+
+    def place_of(zs):
+        return slot_at(z, zs)
+
     def zig(i):
         return zmod(z + jnp.where(lax.rem(i, 2) == 1, (i + 1) // 2, -(i // 2)))
 
@@ -447,59 +453,56 @@
     v_new = arrived(1)
     kv_ref[...] = kvnew[...].reshape(kv_ref.shape)
     mixed = (mixed + dot(w_new.astype(BF16), v_new)) / total
-    gath[z, g] = mixed.astype(BF16)
+    gath[place_of(z), g] = mixed.astype(BF16)
 
     gy_of = (1 - yl) * 2 + co
 
     def ga_copy(i):
-        return rc(gath.at[z, g], gath.at[z, g], ga_s.at[i], ga_r.at[z], (zig(nz - i) * G + g, h))
-
-    def gy_copy(zt):
-        return rc(gath.at[zt, g], gath.at[zt, g], gy_s.at[zt], gy_r.at[zt], y_dev)
-
-    def gc_copy(zt, k):
-        gk = g if k == 0 else gy_of
-        return rc(gath.at[zt, gk], gath.at[zt, gk], gc_s.at[k, zt], gc_r.at[k, zt], core_dev)
+        zt = zig(nz - i)
+        return rc(gath.at[place_of(z), g], gath.at[slot_at(zt, z), g], ga_s.at[i], ga_r.at[slot_at(zt, z)], (zt * G + g, h))
 
     def ga_start(i, _):
         ga_copy(i).start()
         return 0
 
     lax.fori_loop(1, nz, ga_start, 0)
-    gy_copy(z).start()
-    gc_copy(z, 0).start()
-
-    def hand_on(i, _):
-        zt = zig(i)
-        rc(gath.at[zt, g], gath.at[zt, g], ga_s.at[0], ga_r.at[zt], core_dev).wait_recv()
-        gy_copy(zt).start()
-        gc_copy(zt, 0).start()
-        return 0
-
-    def hand_over(i, _):
-        zt = zig(i)
-        rc(gath.at[zt, gy_of], gath.at[zt, gy_of], ga_s.at[0], gy_r.at[zt], core_dev).wait_recv()
-        gc_copy(zt, 1).start()
-        return 0
-
-    def gc_wait(zt, _):
+    batches = ((6, 5), (3, 3), (11, 3), (0, 3), (14, 2)) if nz == 16 else ((0, nz),)
+
+    def gy_copy(b):
+        first, count = batches[b]
+        ref = gath.at[pl.ds(first, count), g]
+        return rc(ref, ref, gy_s.at[b], gy_r.at[b], y_dev)
+
+    def gc_copy(b, k):
+        first, count = batches[b]
+        ref = gath.at[pl.ds(first, count), g if k == 0 else gy_of]
+        return rc(ref, ref, gc_s.at[k, b], gc_r.at[k, b], core_dev)
+
+    for b, (first, count) in enumerate(batches):
+        def ga_wait(i, _):
+            slot = gath.at[i, g]
+            pl.when(i != place_of(z))(rc(slot, slot, ga_s.at[0], ga_r.at[i], core_dev).wait_recv)
+            return 0
+
+        lax.fori_loop(first, first + count, ga_wait, 0)
+        gy_copy(b).start()
+        gc_copy(b, 0).start()
+    for b, (first, count) in enumerate(batches):
+        slot = gath.at[pl.ds(first, count), gy_of]
+        rc(slot, slot, ga_s.at[0], gy_r.at[b], core_dev).wait_recv()
+        gc_copy(b, 1).start()
+    for b, (first, count) in enumerate(batches):
         for k in range(2):
-            slot = gath.at[zt, (yl if k == 0 else 1 - yl) * 2 + 1 - co]
-            rc(slot, slot, ga_s.at[0], gc_r.at[k, zt], core_dev).wait_recv()
-        return 0
-
-    lax.fori_loop(1, nz, hand_on, 0)
-    lax.fori_loop(0, nz, hand_over, 0)
-    lax.fori_loop(0, nz, gc_wait, 0)
+            slot = gath.at[pl.ds(first, count), (yl if k == 0 else 1 - yl) * 2 + 1 - co]
+            rc(slot, slot, ga_s.at[0], gc_r.at[k, b], core_dev).wait_recv()
 
     def ga_done(i, _):
-        pl.when(i > 0)(lambda: ga_copy(i).wait_send())
-        gy_copy(i).wait_send()
-        gc_copy(i, 0).wait_send()
-        gc_copy(i, 1).wait_send()
-        return 0
-
-    pending.append(lambda: lax.fori_loop(0, nz, ga_done, 0))
+        ga_copy(i).wait_send()
+        return 0
+
+    pending.append(lambda: lax.fori_loop(1, nz, ga_done, 0))
+    for b in range(len(batches)):
+        sent(gy_copy(b), gc_copy(b, 0), gc_copy(b, 1))
 
     gf[...] = gath[...].reshape(gf.shape).astype(F32)
     for t in range(steps):
@@ -509,9 +512,12 @@
     obuf[...] = dot(lhs[...], ow_ref[...]).reshape(obuf.shape)
     mine = seqs // nh
 
+    def rows_of(head):
+        return pl.multiple_of(place_of(head * mine // G) * G, mine)
+
     def or_copy(i):
         ht = lax.rem(h + i, nh)
-        src = obuf.at[:, pl.ds(pl.multiple_of(ht * mine, mine), mine), :]
+        src = obuf.at[:, pl.ds(rows_of(ht), mine), :]
         return rc(src, orecv.at[h], or_s.at[i], or_r.at[h], (c, ht))
 
     def or_start(i, _):
@@ -519,7 +525,7 @@
         return 0
 
     lax.fori_loop(1, nh, or_start, 0)
-    orecv[h] = obuf[:, pl.ds(pl.multiple_of(h * mine, mine), mine), :]
+    orecv[h] = obuf[:, pl.ds(rows_of(h), mine), :]
 
     def or_wait(i, _):
         hs = lax.rem(h + i, nh)
@@ -540,15 +546,10 @@
     finish()
 
 
-def place(out_ref, kv_ref, attn_ref, nk_ref, nv_ref, sems):
-    moves = [
-        pltpu.make_async_copy(src, dst, sems.at[i])
-        for i, (src, dst) in enumerate(((kv_ref.at[0], nk_ref.at[0]), (kv_ref.at[1], nv_ref.at[0]), (out_ref, attn_ref)))
-    ]
-    for move in moves:
-        move.start()
-    for move in moves:
-        move.wait()
+def place(out_ref, kv_ref, attn_ref, nk_ref, nv_ref):
+    attn_ref[...] = out_ref[...]
+    nk_ref[0] = kv_ref[0]
+    nv_ref[0] = kv_ref[1]
 
 
 def body(
@@ -611,7 +612,7 @@
             dma, dma, dma((G,)), dma((G,)), dma((G,)), dma((G,)),
             dma, dma, dma, dma, dma((up_n,)), dma((up_n,)), dma((dn_n,)), dma((dn_n,)),
             dma((nh, 2)), dma((nh, 2)), dma((2, nz)), dma((2, nz)), dma((nz,)), dma((nz,)),
-            dma((nz,)), dma((nz,)), dma((2, nz)), dma((2, nz)), dma((nh,)), dma((nh,)),
+            dma((5,)), dma((5,)), dma((2, 5)), dma((2, 5)), dma((nh,)), dma((nh,)),
         ],
         compiler_params=pltpu.CompilerParams(
             collective_id=0, has_side_effects=True, vmem_limit_bytes=60 * 2**20
@@ -625,10 +626,8 @@
             jax.ShapeDtypeStruct((1, nz * pos, hd), BF16),
             jax.ShapeDtypeStruct((1, nz * pos, hd), BF16),
         ),
-        in_specs=[pl.BlockSpec(memory_space=pl.ANY)] * 2,
-        out_specs=(pl.BlockSpec(memory_space=pl.ANY),) * 3,
-        scratch_shapes=[dma((3,))],
-        compiler_params=pltpu.CompilerParams(vmem_limit_bytes=60 * 2**20),
+        in_specs=[vspec] * 2,
+        out_specs=(vspec,) * 3,
         name="place",
     )(out, kv)
 

time: 113 us -> 109 us (0.965)
  Pallas kernels: 112 us -> 108 us
    pallas_call x1, Pallas kernels: 5.35 us -> 1.58 us  [body(): pl.pallas_call(place, out_shape=(jax.ShapeDtypeStruct(out.shape, BF16), j...]
where the time goes in v4:
time: 109 us
  Pallas kernels  108 us (99%)
  between operations  1.29 us (1%)
    pallas_call x1, Pallas kernels, body(): pl.pallas_call(functools.partial(kernel, nz, nh), out_shape=(jax.ShapeDty...  106 us

profile of v4, /device:TPU:1, one launch (start us, length us, event | category | flops | bytes accessed | tf_op | source)
XLA Modules:
  0.0 109.0 jit_solution(996089830349247445)
XLA Ops:
  1.3 106.1 %layer.1 = (bf16[2,8,256]{2,1,0:T(8,128)(2,1)}, bf16[2,256,128]{2,1,0:T(8,128)(2,1)}) custom-call(bf16[4,64,2048]{2,1,0:T(8,128)(2,1)} %span_hbm.1, bf16[256,256]{1,0:T(8,128)(2,1)} %kvw_hbm.1, bf16[256,2048]{1,0:T(8,128)(2,1)} %qw_hbm.1, f32[16,128]{1,0:T(8,128)} %bitcast.8, bf16[2048,256]{1,0:T(8,128)(2,1)} %ow_hbm.1, bf16[128,256]{1,0:T(8,128)(2,1)} %bitcast.5, ...), custom_call_target="tpu_custom_call" | custom-call | tf_op jit(solution)/shard_map/layer/pallas_call | solution.py:581
  107.4 1.6 %place.1 = (bf16[2,8,256]{2,1,0:T(8,128)(2,1)}, bf16[1,256,128]{2,1,0:T(8,128)(2,1)}, bf16[1,256,128]{2,1,0:T(8,128)(2,1)}) custom-call(bf16[2,8,256]{2,1,0:T(8,128)(2,1)} %get-tuple-element.5.out_ref, bf16[2,256,128]{2,1,0:T(8,128)(2,1)} %get-tuple-element.6.kv_ref), custom_call_target="tpu_custom_call" | custom-call | tf_op jit(solution)/shard_map/place/pallas_call | solution.py:622
